TPU v7x, 256 devices: a whole 4x4x8 slice. The times are simulated.
256 devices in a mesh: dp: 128 (over z, x_hi, y, core), fsdp: 2 (over x_lo).
Axes of the slice: x: 4 (x_hi: 2, x_lo: 2; x = x_hi * 2 + x_lo), y: 4, z: 8, core: 2. Of those that a mesh axis runs over, the one named last changes fastest.
Arguments:
- super_image: bfloat16 [81920, 1152], P(('dp', 'fsdp')), may hold values from -0.35 to 0.35
- super_text: bfloat16 [81920, 1152], P(('dp', 'fsdp')), may hold values from -0.35 to 0.35
- selected: int32 [16384], P(('dp', 'fsdp')), may hold values from 0 to 319, as said below
- buckets: int32 [16384], P(('dp', 'fsdp')), may hold values from 0 to 15
- bucket_weights: float32 [16], replicated, may hold values from 3 to 4
- image_proj: bfloat16 [1152, 576], P('fsdp'), may hold values from -0.11785113 to 0.11785113
- text_proj: bfloat16 [1152, 576], P('fsdp'), may hold values from -0.11785113 to 0.11785113
- logit_scale: float32 [1], replicated, may hold values from 5 to 10
- logit_bias: float32 [1], replicated, may hold values from -5 to -2
- loss_scale: float32 [1], replicated, may hold values from 1024 to 8192
Outputs:
- grad_image_proj: float32 [1152, 576], P('fsdp')
- grad_text_proj: float32 [1152, 576], P('fsdp')
- grad_super_image: float32 [81920, 1152], P(('dp', 'fsdp'))
- grad_super_text: float32 [81920, 1152], P(('dp', 'fsdp'))
Inputs may be any that keep to these rules, and one draw needn't show every extreme that they name: `selected`: the 64 entries of each aligned block of 64 (one device's pairs) are distinct.
All inputs are finite; a program needn't handle non-finite values.
Results may differ from a plain program's by a relative error of at most 0.0085.
Values may be sent and summed in bfloat16 or wider, within the bound.
A program may use at most 128 MiB of HBM per device.

v0:
```python
import jax
import jax.numpy as jnp
from jax import lax
from jax.sharding import PartitionSpec as P


def cross(left, right):
    return lax.dot_general(
        left, right, (((1,), (1,)), ((), ())), preferred_element_type=jnp.float32
    )


def down(left, right):
    return lax.dot_general(
        left, right, (((0,), (0,)), ((), ())), preferred_element_type=jnp.float32
    )


def project(rows, weight):
    raw = jnp.dot(rows, weight, preferred_element_type=jnp.float32)
    length = jnp.sqrt(jnp.sum(raw * raw, axis=1, keepdims=True) + 1e-06)
    return (raw / length, length)


def unproject(grad, unit, length):
    return ((grad - unit * jnp.sum(unit * grad, axis=1, keepdims=True)) / length).astype(
        jnp.bfloat16
    )


def pair_grad(logits, row_ids, col_ids, row_coef):
    sign = jnp.where(row_ids[:, None] == col_ids[None, :], 1.0, -1.0).astype(jnp.float32)
    return (-row_coef[:, None] * sign * jax.nn.sigmoid(-sign * logits)).astype(jnp.bfloat16)


def body(
    super_image,
    super_text,
    selected,
    buckets,
    bucket_weights,
    image_proj,
    text_proj,
    logit_scale,
    logit_bias,
    loss_scale,
):
    count = selected.shape[0]
    total = count * lax.axis_size(("dp", "fsdp"))
    width = image_proj.shape[1]
    features = super_image.shape[1]
    image_rows = jnp.take(super_image, selected, axis=0)
    text_rows = jnp.take(super_text, selected, axis=0)
    full_image, full_text = (
        lax.all_gather(image_proj, "fsdp", axis=0, tiled=True),
        lax.all_gather(text_proj, "fsdp", axis=0, tiled=True),
    )
    image_unit, image_len = project(image_rows, full_image)
    text_unit, text_len = project(text_rows, full_text)
    image_emb = image_unit.astype(jnp.bfloat16)
    text_emb = text_unit.astype(jnp.bfloat16)
    levels = jnp.arange(bucket_weights.shape[0], dtype=jnp.int32)
    onehot = (buckets[:, None] == levels[None, :]).astype(jnp.float32)
    coef = loss_scale[0] * jnp.sum(onehot * bucket_weights[None, :], axis=1) / total
    scale = logit_scale[0]
    bias = logit_bias[0]
    local_ids = lax.axis_index(("dp", "fsdp")) * count + jnp.arange(count, dtype=jnp.int32)
    text_piece = lax.all_gather(text_emb, ("dp", "fsdp"), axis=0, tiled=True)
    ids = jnp.arange(text_piece.shape[0], dtype=jnp.int32)
    row_grad = pair_grad(scale * cross(image_emb, text_piece) + bias, local_ids, ids, coef)
    grad_image_emb = scale * jnp.dot(row_grad, text_piece, preferred_element_type=jnp.float32)
    image_piece = lax.all_gather(image_emb, ("dp", "fsdp"), axis=0, tiled=True)
    coef_piece = lax.all_gather(
        coef.astype(jnp.bfloat16), ("dp", "fsdp"), axis=0, tiled=True
    ).astype(jnp.float32)
    ids = jnp.arange(image_piece.shape[0], dtype=jnp.int32)
    col_grad = pair_grad(scale * cross(image_piece, text_emb) + bias, ids, local_ids, coef_piece)
    grad_text_emb = scale * down(col_grad, image_piece)
    image_back = unproject(grad_image_emb, image_unit, image_len)
    text_back = unproject(grad_text_emb, text_unit, text_len)
    share = lax.psum_scatter(
        jnp.concatenate([down(image_rows, image_back), down(text_rows, text_back)], axis=1).astype(
            jnp.bfloat16
        ),
        "fsdp",
        scatter_dimension=0,
        tiled=True,
    ).astype(jnp.float32)
    summed = lax.psum(share, "dp")
    head_image, head_text = (full_image, full_text)
    image_feat = cross(image_back, head_image)
    text_feat = cross(text_back, head_text)
    grad_super_image = (
        jnp.zeros((super_image.shape[0], features), jnp.float32).at[selected].set(image_feat)
    )
    grad_super_text = (
        jnp.zeros((super_text.shape[0], features), jnp.float32).at[selected].set(text_feat)
    )
    return (summed[:, :width], summed[:, width:], grad_super_image, grad_super_text)


def solution(mesh):
    in_specs = (
        P(("dp", "fsdp"), None),
        P(("dp", "fsdp"), None),
        P(("dp", "fsdp")),
        P(("dp", "fsdp")),
        P(),
        P("fsdp", None),
        P("fsdp", None),
        P(),
        P(),
        P(),
    )
    out_specs = (P("fsdp", None), P("fsdp", None), P(("dp", "fsdp"), None), P(("dp", "fsdp"), None))
    return jax.shard_map(body, mesh=mesh, in_specs=in_specs, out_specs=out_specs, check_vma=False)
```

profile of v0, /device:TPU:2, one launch (start us, length us, event | category | flops | bytes accessed | tf_op | source)
XLA Modules:
  0.0 2331.9 jit_solution(7258451964313391699)
XLA Ops:
  7.2 0.0 copy-start
  7.2 0.0 copy-start.2
  7.2 0.0 copy-start.8
  7.2 0.0 copy-start.9
  7.2 0.0 all-gather.7.cloned.1.call-start
  7.3 0.7 all-gather.7.cloned.1.call-update
  7.9 0.0 all-gather.5.cloned.1.call-start
  8.0 0.7 all-gather.5.cloned.1.call-update
  8.7 0.0 all-gather.9.cloned.1.call-start
  8.7 0.7 compare_select_fusion
  9.4 0.5 copy-done.5
  10.0 0.7 gather_fusion.1
  10.7 0.7 compare_and_fusion
  11.4 31.5 %all-gather.7.cloned.1.call-done = bf16[1152,576]{1,0:T(8,128)(2,1)} async-done(((bf16[576,576]{1,0:T(8,128)(2,1)}), bf16[1152,576]{1,0:T(8,128)(2,1)}) %all-gather.7.cloned.1.call-update) | async-done | bytes 1327120 | tf_op jit(solution)/shard_map/all_gather | solution.py:56
  42.9 1.9 multiply_reduce_fusion.2
  44.8 0.7 fusion.43
  45.5 0.0 all-gather.9.cloned.1.call-update
  45.5 0.0 all-gather.11.cloned.1.call-start
  45.6 0.0 copy-done.2
  45.6 0.7 gather_fusion
  46.3 30.5 %all-gather.5.cloned.1.call-done = bf16[1152,576]{1,0:T(8,128)(2,1)} async-done(((bf16[576,576]{1,0:T(8,128)(2,1)}), bf16[1152,576]{1,0:T(8,128)(2,1)}) %all-gather.5.cloned.1.call-update) | async-done | bytes 1327120 | tf_op jit(solution)/shard_map/all_gather | solution.py:55
  76.8 1.9 multiply_reduce_fusion.3
  78.8 0.7 fusion.42
  79.5 0.0 all-gather.11.cloned.1.call-update
  79.5 0.0 reduce-scatter.4.cloned.1.call-start
  81.5 0.1 select_reduce_fusion
  81.6 0.2 dynamic-update-slice
  81.9 76.9 %all-reduce = bf16[16384]{0:T(1024)(128)(2,1)S(1)} all-reduce(bf16[16384]{0:T(1024)(128)(2,1)S(1)} %dynamic-update-slice), channel_id=1, replica_groups=mesh['dp'=128,'fsdp'=2] {'dp','fsdp'}, use_global_device_ids=true, to_apply=%add | all-reduce | flops 16384 | bytes 65536
  158.8 660.1 %all-gather.9.cloned.1.call-done = bf16[16384,576]{1,0:T(8,128)(2,1)} async-done(((bf16[64,576]{1,0:T(8,128)(2,1)}), bf16[16384,576]{1,0:T(8,128)(2,1)}) %all-gather.9.cloned.1.call-update) | async-done | bytes 18874384 | tf_op jit(solution)/shard_map/all_gather | solution.py:68
  818.9 21.4 multiply_reduce_fusion.1
  840.3 1.7 convolution_convert_fusion.1
  842.0 718.9 %all-gather.11.cloned.1.call-done = bf16[16384,576]{1,0:T(8,128)(2,1)} async-done(((bf16[64,576]{1,0:T(8,128)(2,1)}), bf16[16384,576]{1,0:T(8,128)(2,1)}) %all-gather.11.cloned.1.call-update) | async-done | bytes 18874384 | tf_op jit(solution)/shard_map/all_gather | solution.py:72
  1560.9 0.0 copy-done.4
  1560.9 23.4 %multiply_reduce_fusion = (f32[64]{0:T(128)S(1)}, f32[64,576]{1,0:T(8,128)S(1)}) fusion(f32[64,576]{1,0:T(8,128)S(1)} %get-tuple-element.28, f32[64]{0:T(128)S(1)} %add_sqrt_fusion, bf16[16384,576]{1,0:T(8,128)(2,1)} %all-gather.11.cloned.1.call-done, bf16[64,576]{1,0:T(8,128)(2,1)S(1)} %copy-done.4, f32[]{:T(128)} %bitcast.17, f32[]{:T(128)} %bitcast.14, ...), kind=kOutput, calls=%fused_computation.46 | convolution fusion | flops 2428649472 | bytes 19309320 | tf_op jit(solution)/shard_map/dot_general | solution.py:14
  1584.3 0.6 convolution_convert_fusion
  1584.9 1.5 pad_maximum_fusion
  1586.5 3.3 copy.22
  1589.8 0.0 reduce-scatter.4.cloned.1.call-update
  1589.8 2.1 fusion.44
  1591.9 2.1 scatter_custom_fusion
  1594.0 0.6 fusion.45
  1594.6 2.1 scatter_custom_fusion.1
  1596.7 37.4 %reduce-scatter.4.cloned.1.call-done = bf16[576,1152]{1,0:T(8,128)(2,1)} async-done(((bf16[1152,1152]{1,0:T(8,128)(2,1)}), bf16[576,1152]{1,0:T(8,128)(2,1)}) %reduce-scatter.4.cloned.1.call-update) | async-done | bytes 1327120
  1634.1 2.1 copy.23
  1636.2 681.4 %all-reduce.2 = f32[576,1152]{0,1:T(8,128)} all-reduce(bf16[576,1152]{0,1:T(8,128)(2,1)S(1)} %copy.23), channel_id=1, replica_groups=mesh['dp'=128,'fsdp'=2] {'dp'}, use_global_device_ids=true, to_apply=%region_6.8 | all-reduce | flops 663552 | bytes 3981312 | tf_op jit(solution)/shard_map/psum | solution.py:89
  2317.6 3.2 fusion.46
  2320.8 3.0 copy.21
  2323.8 1.6 copy.20
  (20 shorter events, 0.1 us)
Async XLA Ops:
  7.2 2.8 copy-start
  7.2 38.4 %copy-start.2 = (bf16[320,1152]{1,0:T(8,128)(2,1)S(1)}, bf16[320,1152]{1,0:T(8,128)(2,1)}, u32[]{:S(2)}) copy-start(bf16[320,1152]{1,0:T(8,128)(2,1)} %param.12) | copy-start | bytes 2211844
  7.2 74.3 %copy-start.8 = (f32[16]{0:T(128)S(1)}, f32[16]{0:T(128)}, u32[]{:S(2)}) copy-start(f32[16]{0:T(128)} %param.16) | copy-start | bytes 196
  7.2 74.3 %copy-start.9 = (s32[64]{0:T(128)S(1)}, s32[64]{0:T(128)}, u32[]{:S(2)}) copy-start(s32[64]{0:T(128)} %param.15) | copy-start | bytes 772
  7.2 35.6 %all-gather.7.cloned.1.call-start = ((), (), s32[]{:S(2)}) async-start(), calls=%async_computation.2 | async-start | bytes 2211840 | tf_op jit(solution)/shard_map/all_gather | solution.py:56
  7.9 68.9 %all-gather.5.cloned.1.call-start = ((), (), s32[]{:S(2)}) async-start(), calls=%async_computation.1 | async-start | bytes 2211840 | tf_op jit(solution)/shard_map/all_gather | solution.py:55
  8.7 810.2 %all-gather.9.cloned.1.call-start = ((), (), s32[]{:S(2)}) async-start(), calls=%async_computation.3 | async-start | bytes 21053440 | tf_op jit(solution)/shard_map/all_gather | solution.py:68
  9.4 0.5 copy-start.5
  45.5 1515.4 %all-gather.11.cloned.1.call-start = ((), (), s32[]{:S(2)}) async-start(), calls=%async_computation.4 | async-start | bytes 21053440 | tf_op jit(solution)/shard_map/all_gather | solution.py:72
  79.5 1554.6 %reduce-scatter.4.cloned.1.call-start = ((), (), s32[]{:S(2)}) async-start(), calls=%async_computation.5 | async-start | bytes 3981312
  818.9 741.9 %copy-start.4 = (bf16[64,576]{1,0:T(8,128)(2,1)S(1)}, bf16[64,576]{1,0:T(8,128)(2,1)}, u32[]{:S(2)}) copy-start(bf16[64,576]{1,0:T(8,128)(2,1)} %fusion.43) | copy-start | bytes 221188
  840.3 744.0 %copy-start.6 = (f32[64]{0:T(128)}, f32[64]{0:T(128)S(1)}, u32[]{:S(2)}) copy-start(f32[64]{0:T(128)S(1)} %get-tuple-element.31) | copy-start | bytes 772
  1586.5 3.3 copy-start.7
  1589.8 4.2 copy-start.3
  2317.6 7.8 copy-start.1
Sparse Core Ops, SparseCore 0:
  9.8 32.9 all-gather.6
  44.6 32.1 all-gather.4
  79.3 739.5 all-gather.8
  821.2 739.5 all-gather.10
  1589.9 44.1 reduce-scatter.3
where the time goes:
time: 2330 us
  waiting for transfers between devices  1480 us (64%)
  blocking collectives  758 us (33%)
  matrix products  53.6 us (2%)
    all_gather x1, waiting for transfers between devices, body(): image_piece = lax.all_gather(image_emb, ('dp', 'fsdp'), axis=0, tiled=True)  719 us
    psum x1, blocking collectives, body(): summed = lax.psum(share, 'dp')  681 us
    all_gather x1, waiting for transfers between devices, body(): text_piece = lax.all_gather(text_emb, ('dp', 'fsdp'), axis=0, tiled=True)  660 us
    unnamed x1, blocking collectives  76.9 us
  transfers between devices with their start and end apart: 5, of which 5 were waited for; matrix products, arithmetic and copies ran while one was open for 2% of the time, Pallas kernels for 0%

commit v1 on v0

v1 whole, which is shorter than its diff:
```python
import functools

import jax
import jax.numpy as jnp
from jax import lax
from jax.experimental import pallas as pl
from jax.experimental.pallas import tpu as pltpu
from jax.sharding import PartitionSpec as P

MESH = pl.DeviceIdType.MESH
BF = jnp.bfloat16
F32 = jnp.float32
NX, NY, NZ = 4, 4, 8
PLANE = NX * NY
PAIRS = 16384
N = 64
N2 = 2 * N
S = 320
D = 1152
H = D // 2
E = 576
EP = 640
PIECE = D // PLANE
PR = 80
NB = 16


def place():
    dp, x_lo = lax.axis_index("dp"), lax.axis_index("fsdp")
    core = lax.rem(dp, 2)
    y = lax.rem(lax.div(dp, 2), NY)
    x = lax.rem(lax.div(dp, 2 * NY), 2) * 2 + x_lo
    z = lax.div(dp, 4 * NY)
    return x, y, z, core


def device(x, y, z, core):
    return (((z * 2 + lax.div(x, 2)) * NY + y) * 2 + core, lax.rem(x, 2))


def dot(a, b, contract):
    return lax.dot_general(a, b, (contract, ((), ())), preferred_element_type=F32)


def kernel(
    sup_i, sup_t, sel, bkt, wts, head_i, head_t, lscale, lbias, oscale,
    gs, gw,
    a, stage, cbuf, wfull, wother, unit, length,
    em, img, txt, g, p_f, p_out, p_in, t_out, rs_i, rs_t,
    bk, bo, gsv, dwf, dws, r1, psum, r2, fin, res,
    w_s, w_r, rows_s, rows_r, c_s, c_r, wo_s, wo_r,
    ia_s, ia_r, if_s, ta_s, ta_r, pi_s, pi_r, ri_s, ri_r, rt_s, rt_r,
    bk_s, bk_r, gs_s, r1_s, r1_r, r2_s, r2_r, f_s, f_r, own_s, ag_s, ag_r, ad_s, ad_r,
):
    x, y, z, core = place()
    half = lax.rem(x, 2)
    sib = device(x, y, z, 1 - core)
    first = core == 0

    def line(k, c=core):
        return device(x, y, lax.rem(z + k, NZ), c)

    def plane(k, c=core):
        return device(lax.rem(x + k // NY, NX), lax.rem(y + k % NY, NY), z, c)

    def back_slot(k):
        return (-(k // NY)) % NX * NY + (-(k % NY)) % NY

    def remote(src, dst, send, recv, to):
        return pltpu.make_async_remote_copy(
            src_ref=src, dst_ref=dst, send_sem=send, recv_sem=recv,
            device_id=to, device_id_type=MESH,
        )

    def arrived(dst, recv, send):
        remote(dst, dst, send, recv, sib).wait_recv()

    def rows(ref, start, count):
        return ref.at[pl.ds(start, count), :]

    barrier = pltpu.get_barrier_semaphore()

    def greet(to):
        pl.semaphore_signal(barrier, inc=1, device_id=to, device_id_type=MESH)

    greet(sib)
    for k in range(1, NZ):
        greet(line(k))
    for k in range(1, PLANE):
        greet(plane(k, 0))
        greet(plane(k, 1))

    h_off = pl.multiple_of(half * H, H)
    wfull[pl.ds(h_off, H), :] = jnp.where(first, head_i[...], head_t[...])
    onehot = (lax.broadcasted_iota(jnp.int32, (S, N), 0) == sel[...]).astype(BF)
    rows_i = dot(onehot, sup_i[...], ((0,), (0,))).astype(BF)
    rows_t = dot(onehot, sup_t[...], ((0,), (0,))).astype(BF)
    mine = pl.multiple_of(core * N, N)
    a[pl.ds(mine, N), :] = jnp.where(first, rows_i, rows_t)
    stage[...] = jnp.where(first, rows_t, rows_i)
    weight = jnp.zeros((1, N), F32)
    for n in range(NB):
        weight = jnp.where(bkt[...] == n, wts[n], weight)
    weight = oscale[0] * weight / PAIRS
    cbuf[pl.ds(pl.multiple_of(core * 8, 8), 8), :] = jnp.concatenate(
        [jnp.broadcast_to(weight, (8, N)), jnp.zeros((8, N), F32)], axis=1
    )

    pl.semaphore_wait(barrier, 1 + (NZ - 1) + 2 * (PLANE - 1))

    heads = []
    for k, step in ((0, 1), (1, NX - 1)):
        src = rows(wfull, pl.multiple_of(h_off + k * (H // 2), H // 2), H // 2)
        heads.append(
            remote(src, src, w_s.at[k], w_r.at[k], device(lax.rem(x + step, NX), y, z, core))
        )
    rows_copy = remote(stage, rows(a, mine, N), rows_s, rows_r, sib)
    c_own = rows(cbuf, pl.multiple_of(core * 8, 8), 8)
    c_copy = remote(c_own, c_own, c_s, c_r, sib)
    for copy in heads:
        copy.start()
    rows_copy.start()
    c_copy.start()
    theirs = pl.multiple_of((1 - core) * N, N)
    o_off = pl.multiple_of((1 - half) * H, H)
    arrived(rows(a, theirs, N), rows_r, rows_s)
    arrived(rows(cbuf, pl.multiple_of((1 - core) * 8, 8), 8), c_r, c_s)
    for k in range(2):
        arrived(
            rows(wfull, pl.multiple_of(o_off + k * (H // 2), H // 2), H // 2), w_r.at[k], w_s.at[k]
        )

    raw = dot(a[...], wfull[...], ((1,), (0,)))
    size = jnp.sqrt(jnp.sum(raw * raw, axis=1, keepdims=True) + 1e-06)
    u = raw / size
    unit[...] = u
    length[...] = jnp.broadcast_to(size, (N2, 128))
    eye = lax.broadcasted_iota(jnp.int32, (N, N), 0) == lax.broadcasted_iota(jnp.int32, (N, N), 1)
    column = jnp.concatenate(
        [
            jnp.sum(jnp.where(eye, cbuf[8 * c : 8 * c + 1, 0:N], 0.0), axis=1, keepdims=True)
            for c in range(2)
        ],
        axis=0,
    )
    column = jnp.where(first, column, jnp.zeros_like(column))
    high = column.astype(BF)
    low = (column - high.astype(F32)).astype(BF)
    em[...] = jnp.concatenate([u.astype(BF), high, low, jnp.zeros((N2, EP - E - 2), BF)], axis=1)

    line_order = (1, 7, 2, 6, 3, 5, 4)
    plane_order = sorted(
        range(1, PLANE),
        key=lambda k: (min(k // 4, 4 - k // 4) + min(k % 4, 4 - k % 4), k),
    )

    def ia(k):
        return remote(
            em, rows(img, (NZ - k) % NZ * N2, N2), ia_s.at[k], ia_r.at[(NZ - k) % NZ], line(k)
        )

    def fwd(s):
        block = rows(img, s * N2, N2)
        src = em if s == 0 else block
        return remote(src, block, if_s.at[s], ia_r.at[s], sib)

    def ta(k, c):
        return remote(
            rows(em, c * N, N), rows(txt, back_slot(k) * N, N),
            ta_s.at[2 * k + c], ta_r.at[back_slot(k)], plane(k, c),
        )

    @pl.when(first)
    def _():
        for k in line_order:
            ia(k).start()
        fwd(0).start()
        img[0:N2, :] = em[...]

    @pl.when(core == 1)
    def _():
        for k in plane_order:
            ta(k, 0).start()
            ta(k, 1).start()
        ta(0, 0).start()
        txt[0:N, :] = em[N:N2, :]

    wo_copy = remote(wfull, wother, wo_s, wo_r, sib)
    wo_copy.start()

    @pl.when(first)
    def _():
        arrived(rows(txt, 0, N), ta_r.at[0], ta_s.at[0])

    for k in plane_order:
        arrived(rows(txt, k * N, N), ta_r.at[k], ta_s.at[0])

    scale = lscale[0]
    neg_scale, neg_bias = -lscale[0], -lbias[0]

    def image_block(s):
        block = img[pl.ds(pl.multiple_of(s * N2, N2), N2), :]
        weight = block[:, E : E + 1].astype(F32) + block[:, E + 1 : E + 2].astype(F32)
        e = jnp.exp(neg_scale * dot(block, txt[...], ((1,), (1,))) + neg_bias)
        positive = weight / (1.0 + e)
        return e, positive

    def take(s):
        @pl.when(first)
        def _():
            if s:
                arrived(rows(img, s * N2, N2), ia_r.at[s], ia_s.at[0])
                fwd(s).start()

        @pl.when(core == 1)
        def _():
            arrived(rows(img, s * N2, N2), ia_r.at[s], ia_s.at[0])

    for s in (0,) + line_order:
        take(s)
        e, positive = image_block(s)
        if s == 0:
            r = lax.broadcasted_iota(jnp.int32, (N2, PLANE * N), 0)
            c = lax.broadcasted_iota(jnp.int32, (N2, PLANE * N), 1)
            same = (r == c + core * N) & (c < N)
            positive = jnp.where(same, -positive * e, positive)
        g[s * N2 : (s + 1) * N2, :] = positive.astype(BF)

    def partial_i(s):
        off = pl.multiple_of(s * N2, N2)
        return dot(g[pl.ds(off, N2), :], txt[:, 0:E], ((1,), (0,)))

    def pi(s):
        return remote(rows(p_out, s * N2, N2), rows(p_in, s * N2, N2), pi_s.at[s], pi_r.at[s], sib)

    def ri(k):
        return remote(
            rows(p_out, k * N2, N2), rows(rs_i, (NZ - k) % NZ * N2, N2),
            ri_s.at[k], ri_r.at[(NZ - k) % NZ], line(k),
        )

    def wait_fwd(s):
        fwd(s).wait_send()

    @pl.when(first)
    def _():
        for k in line_order:
            ia(k).wait_send()
        for s in range(NZ):
            wait_fwd(s)

    @pl.when(core == 1)
    def _():
        for k in plane_order:
            ta(k, 0).wait_send()
            ta(k, 1).wait_send()
        ta(0, 0).wait_send()

    send_order = line_order + (0,)
    for s in send_order:
        p_f[s * N2 : (s + 1) * N2, :] = partial_i(s)

        @pl.when(core == 1)
        def _(s=s):
            p_out[s * N2 : (s + 1) * N2, :] = p_f[s * N2 : (s + 1) * N2, :].astype(BF)
            pi(s).start()

    @pl.when(first)
    def _():
        for s in send_order:
            arrived(rows(p_in, s * N2, N2), pi_r.at[s], pi_s.at[s])
            total = p_f[s * N2 : (s + 1) * N2, :] + p_in[s * N2 : (s + 1) * N2, :].astype(F32)
            if s:
                p_out[s * N2 : (s + 1) * N2, :] = total.astype(BF)
                ri(s).start()
            else:
                p_f[0:N2, :] = total

    def rt(k):
        return remote(
            rows(t_out, k * N, N), rows(rs_t, (core * PLANE + back_slot(k)) * N, N),
            rt_s.at[k], rt_r.at[core * PLANE + back_slot(k)], plane(k, 1),
        )

    for b in range(PLANE // 2):
        block = dot(g[:, b * N2 : (b + 1) * N2], img[:, 0:E], ((0,), (0,)))
        t_out[b * N2 : (b + 1) * N2, :] = block.astype(BF)
        for k in (2 * b, 2 * b + 1):
            if k:
                rt(k).start()
            else:

                @pl.when(first)
                def _():
                    rt(0).start()

                @pl.when(core == 1)
                def _(block=block):
                    p_f[N : 2 * N, :] = block[0:N, :]

    @pl.when(core == 1)
    def _():
        arrived(rows(rs_t, 0, N), rt_r.at[0], rt_s.at[0])
        p_f[0:N, :] = rs_t[0:N, :].astype(F32)
        for k in plane_order:
            for c in range(2):
                at = c * PLANE + k
                arrived(rows(rs_t, at * N, N), rt_r.at[at], rt_s.at[0])
                p_f[c * N : (c + 1) * N, :] += rs_t[at * N : (at + 1) * N, :].astype(F32)

    @pl.when(first)
    def _():
        for s in line_order:
            arrived(rows(rs_i, s * N2, N2), ri_r.at[s], ri_s.at[0])
            p_f[0:N2, :] += rs_i[s * N2 : (s + 1) * N2, :].astype(F32)

    grad = p_f[0:N2, :] * scale
    u = unit[...]
    back = ((grad - u * jnp.sum(u * grad, axis=1, keepdims=True)) / length[:, 0:1]).astype(BF)
    bk[...] = back
    bk_copy = remote(rows(bk, theirs, N), bo, bk_s, bk_r, sib)
    bk_copy.start()

    dwf[...] = dot(a[...], back, ((0,), (0,)))

    def piece(px, py):
        return (lax.rem(px, 2) * 2 + lax.div(px, 2)) * NY + py

    def r1_copy(k):
        return remote(
            rows(dws, k * PR, PR), rows(r1, back_slot(k) * PR, PR),
            r1_s.at[k], r1_r.at[back_slot(k)], plane(k),
        )

    def part(k):
        q = piece(lax.rem(x + k // NY, NX), lax.rem(y + k % NY, NY))
        return dwf[pl.ds(pl.multiple_of(q * PIECE, 8), PIECE), :]

    for k in plane_order:
        dws[k * PR : (k + 1) * PR, :] = jnp.concatenate(
            [part(k), jnp.zeros((PR - PIECE, E), F32)], axis=0
        ).astype(BF)
        r1_copy(k).start()

    arrived(bo, bk_r, bk_s)
    arrived(wother, wo_r, wo_s)
    own = bk[pl.ds(mine, N), :]
    moved = dot(onehot, own, ((1,), (0,))).astype(BF)
    gsv[core] = dot(moved, wfull[...], ((1,), (1,)))
    moved = dot(onehot, bo[...], ((1,), (0,))).astype(BF)
    gsv[1 - core] = dot(moved, wother[...], ((1,), (1,)))
    gs_copy = pltpu.make_async_copy(gsv, gs, gs_s)
    gs_copy.start()

    total = part(0)
    for k in plane_order:
        arrived(rows(r1, k * PR, PR), r1_r.at[k], r1_s.at[k])
        total += r1[k * PR : (k + 1) * PR, :].astype(F32)[0:PIECE, :]
    whole = jnp.concatenate([total, jnp.zeros((PR - PIECE, E), F32)], axis=0)
    psum[...] = whole.astype(BF)

    rank = lax.rem(z + 4 * core, NZ)

    def rank_of(k):
        return lax.rem(rank + k, NZ)

    def tile(ref, at, base=0):
        return rows(ref, pl.multiple_of(base + at * 16, 16), 16)

    def r2_copy(k):
        back_k = (NZ - k) % NZ
        return remote(
            tile(psum, rank_of(k)), rows(r2, back_k * 16, 16), r2_s.at[k], r2_r.at[back_k], line(k)
        )

    for k in line_order:

        @pl.when(rank_of(k) < 5)
        def _(k=k):
            r2_copy(k).start()

    def f_copy(k):
        return remote(res, tile(fin, rank), f_s.at[k], f_r.at[(NZ - k) % NZ], line(k))

    @pl.when(rank < 5)
    def _():
        total = psum[pl.ds(pl.multiple_of(rank * 16, 16), 16), :].astype(F32)
        for k in line_order:
            arrived(rows(r2, k * 16, 16), r2_r.at[k], r2_s.at[k])
            total += r2[k * 16 : (k + 1) * 16, :].astype(F32)
        res[...] = total.astype(BF)
        for k in line_order:
            f_copy(k).start()
        fin[pl.ds(pl.multiple_of(rank * 16, 16), 16), :] = total.astype(BF)

    for k in line_order:

        @pl.when(rank_of(k) < 5)
        def _(k=k):
            arrived(tile(fin, rank_of(k)), f_r.at[k], f_s.at[k])

    def held(px, py):
        return pl.multiple_of((lax.div(px, 2) * NY + py) * PR, PR)

    mates = [k for k in plane_order if (k // NY) % 2 == 0]

    def mate(k):
        return lax.rem(x + k // NY, NX), lax.rem(y + k % NY, NY)

    def ag_copy(k):
        return remote(
            fin, gw.at[core, pl.ds(held(x, y), PR), :],
            ag_s.at[k], ag_r.at[back_slot(k)], plane(k),
        )

    def ad_copy(k):
        block = gw.at[core, pl.ds(held(*mate(k)), PR), :]
        return remote(fin if k == 0 else block, block, ad_s.at[k], ad_r.at[k], sib)

    for k in mates:
        ag_copy(k).start()
    ad_copy(0).start()
    own_copy = pltpu.make_async_copy(fin, gw.at[core, pl.ds(held(x, y), PR), :], own_s)
    own_copy.start()
    for k in mates:
        arrived(gw.at[core, pl.ds(held(*mate(k)), PR), :], ag_r.at[k], ag_s.at[k])
        ad_copy(k).start()
    for k in [0] + mates:
        arrived(gw.at[1 - core, pl.ds(held(*mate(k)), PR), :], ad_r.at[k], ad_s.at[k])

    for copy in heads + [rows_copy, c_copy, wo_copy, bk_copy]:
        copy.wait_send()

    @pl.when(first)
    def _():
        for k in line_order:
            ri(k).wait_send()
        rt(0).wait_send()

    @pl.when(core == 1)
    def _():
        for s in range(NZ):
            pi(s).wait_send()

    for k in plane_order:
        rt(k).wait_send()
        r1_copy(k).wait_send()
    for k in line_order:

        @pl.when(rank_of(k) < 5)
        def _(k=k):
            r2_copy(k).wait_send()

    @pl.when(rank < 5)
    def _():
        for k in line_order:
            f_copy(k).wait_send()

    for k in mates:
        ag_copy(k).wait_send()
    for k in [0] + mates:
        ad_copy(k).wait_send()
    own_copy.wait()
    gs_copy.wait()


def body(sup_i, sup_t, selected, buckets, weights, head_i, head_t, lscale, lbias, oscale):
    vmem = pl.BlockSpec(memory_space=pltpu.VMEM)
    smem = pl.BlockSpec(memory_space=pltpu.SMEM)
    hbm = pl.BlockSpec(memory_space=pl.ANY)

    def space(shape, dtype=BF):
        return pltpu.VMEM(shape, dtype)

    dma = pltpu.SemaphoreType.DMA
    buffers = [
        space((N2, D)), space((N, D)), space((16, 128), F32), space((D, E)), space((D, E)),
        space((N2, E), F32), space((N2, 128), F32),
        space((N2, EP)), space((NZ * N2, EP)), space((PLANE * N, EP)),
        space((NZ * N2, PLANE * N)),
        space((NZ * N2, E), F32), space((NZ * N2, E)), space((NZ * N2, E)), space((PLANE * N, E)),
        space((NZ * N2, E)), space((2 * PLANE * N, E)),
        space((N2, E)), space((N, E)), space((2, S, D), F32), space((D, E), F32),
        space((PLANE * PR, E)), space((PLANE * PR, E)), space((PR, E)), space((NZ * 16, E)),
        space((PR, E)), space((16, E)),
    ]
    counts = [
        2, 2, 0, 0, 0, 0, 0, 0,
        NZ, NZ, NZ, 2 * PLANE, PLANE, NZ, NZ, NZ, NZ, PLANE, 2 * PLANE,
        0, 0, 0, PLANE, PLANE, NZ, NZ, NZ, NZ, 0, PLANE, PLANE, PLANE, PLANE,
    ]
    sems = [dma((n,)) if n else dma for n in counts]
    gs, gw = pl.pallas_call(
        kernel,
        out_shape=(
            jax.ShapeDtypeStruct((2, S, D), F32),
            jax.ShapeDtypeStruct((2, 8 * PR, E), BF),
        ),
        in_specs=[vmem] * 4 + [smem] + [vmem] * 2 + [smem] * 3,
        out_specs=(hbm, hbm),
        scratch_shapes=buffers + sems,
        compiler_params=pltpu.CompilerParams(
            collective_id=0, has_side_effects=True, vmem_limit_bytes=56 * 1024 * 1024
        ),
    )(
        sup_i, sup_t, selected.reshape(1, N), buckets.reshape(1, N), weights,
        head_i, head_t, lscale, lbias, oscale,
    )
    gw = gw.reshape(2, 8, PR, E)[:, :, 0:PIECE, :].reshape(2, H, E).astype(F32)
    return gw[0], gw[1], gs[0], gs[1]


def solution(mesh):
    both = P(("dp", "fsdp"))
    wide = P(("dp", "fsdp"), None)
    head = P("fsdp", None)
    in_specs = (wide, wide, both, both, P(), head, head, P(), P(), P())
    out_specs = (head, head, wide, wide)
    return jax.shard_map(body, mesh=mesh, in_specs=in_specs, out_specs=out_specs, check_vma=False)
```

time: 2330 us -> 129 us (0.06)
  the two profiles are of different devices: /device:TPU:2 before, /device:TPU:35 now
where the time goes in v1:
time: 129 us; the launch traced here: 128 us
  Pallas kernels  119 us (92%)
  local copies, waits for them, and re-layouts  4.67 us (4%)
  between operations  2.59 us (2%)
  other arithmetic  1.57 us (1%)
    pallas_call x1, Pallas kernels, body(): pl.pallas_call(kernel, out_shape=(jax.ShapeDtypeStruct((2, S, D), F32), j...  119 us

profile of v1, /device:TPU:35, one launch (start us, length us, event | category | flops | bytes accessed | tf_op | source)
XLA Modules:
  0.0 128.0 jit_solution(18220811853759718879)
XLA Ops:
  2.6 119.2 %shard_map.129 = (f32[2,320,1152]{2,1,0:T(8,128)}, bf16[2,640,576]{2,1,0:T(8,128)(2,1)}) custom-call(bf16[320,1152]{1,0:T(8,128)(2,1)} %sup_i.1, bf16[320,1152]{1,0:T(8,128)(2,1)} %sup_t.1, s32[1,64]{1,0:T(1,128)} %bitcast.12, s32[1,64]{1,0:T(1,128)} %bitcast.13, f32[16]{0:T(128)} %wts.1, bf16[576,576]{1,0:T(8,128)(2,1)} %head_i.1, bf16[576,576]{1,0:T(8,128)(2,1)} %head_t.1, ...), custom_call_target="tpu_custom_call" | custom-call | tf_op jit(solution)/shard_map/pallas_call | solution.py:493
  121.8 1.6 %slice_convert_fusion = f32[2,8,72,576]{3,2,1,0:T(8,128)S(1)} fusion(bf16[2,8,80,576]{3,2,1,0:T(8,128)(2,1)} %bitcast.11), kind=kLoop, calls=%fused_computation | loop fusion | flops 663552 | bytes 3981312 | tf_op jit(solution)/shard_map/convert_element_type | solution.py:509
  123.4 0.0 copy-start
  123.4 1.8 %fusion = (f32[1,8,72,576]{3,2,1,0:T(8,128)}, f32[1,8,72,576]{3,2,1,0:T(8,128)}) fusion(f32[2,8,72,576]{3,2,1,0:T(8,128)S(1)} %slice_convert_fusion), kind=kLoop, calls=%fused_computation.3 | loop fusion | bytes 5308416 | tf_op jit(solution)/shard_map/slice | solution.py:510
  125.2 1.1 copy-done
  126.3 1.8 %slice_bitcast_fusion = (f32[320,1152]{1,0:T(8,128)}, f32[320,1152]{1,0:T(8,128)}) fusion(f32[2,320,1152]{2,1,0:T(8,128)S(1)} %copy-done), kind=kLoop, calls=%fused_computation.1 | loop fusion | bytes 5898240 | tf_op jit(solution)/shard_map/squeeze | solution.py:510
Async XLA Ops:
  123.4 2.9 %copy-start = (f32[2,320,1152]{2,1,0:T(8,128)S(1)}, f32[2,320,1152]{2,1,0:T(8,128)}, u32[]{:S(2)}) copy-start(f32[2,320,1152]{2,1,0:T(8,128)} %get-tuple-element.7) | copy-start | bytes 8847364

commit v2 on v1

--- a/solution.py
+++ b/solution.py
@@ -21,8 +21,22 @@
 E = 576
 EP = 640
 PIECE = D // PLANE
+B = 256
 PR = 80
 NB = 16
+LOG2E = 1.4426950408889634
+
+
+def hops(k):
+    return min(k // NY, NX - k // NY) + min(k % NY, NY - k % NY)
+
+
+def back_slot(k):
+    return (-(k // NY)) % NX * NY + (-(k % NY)) % NY
+
+
+LINE = (0, 1, 7, 2, 6, 3, 5, 4)
+SHEET = tuple(sorted(range(PLANE), key=lambda k: (hops(k), k)))
 
 
 def place():
@@ -44,11 +58,11 @@
 
 def kernel(
     sup_i, sup_t, sel, bkt, wts, head_i, head_t, lscale, lbias, oscale,
-    gs, gw,
-    a, stage, cbuf, wfull, wother, unit, length,
+    gs_i, gs_t, gw,
+    va, vt, a, stage, cbuf, wfull, wother, unit, length,
     em, img, txt, g, p_f, p_out, p_in, t_out, rs_i, rs_t,
     bk, bo, gsv, dwf, dws, r1, psum, r2, fin, res,
-    w_s, w_r, rows_s, rows_r, c_s, c_r, wo_s, wo_r,
+    in_s, w_s, w_r, rows_s, rows_r, c_s, c_r, wo_s, wo_r,
     ia_s, ia_r, if_s, ta_s, ta_r, pi_s, pi_r, ri_s, ri_r, rt_s, rt_r,
     bk_s, bk_r, gs_s, r1_s, r1_r, r2_s, r2_r, f_s, f_r, own_s, ag_s, ag_r, ad_s, ad_r,
 ):
@@ -63,9 +77,6 @@
     def plane(k, c=core):
         return device(lax.rem(x + k // NY, NX), lax.rem(y + k % NY, NY), z, c)
 
-    def back_slot(k):
-        return (-(k // NY)) % NX * NY + (-(k % NY)) % NY
-
     def remote(src, dst, send, recv, to):
         return pltpu.make_async_remote_copy(
             src_ref=src, dst_ref=dst, send_sem=send, recv_sem=recv,
@@ -82,6 +93,23 @@
 
     def greet(to):
         pl.semaphore_signal(barrier, inc=1, device_id=to, device_id_type=MESH)
+
+    h_off = pl.multiple_of(half * H, H)
+    sup_copies = [
+        pltpu.make_async_copy(sup_i, va, in_s.at[0]),
+        pltpu.make_async_copy(sup_t, vt, in_s.at[1]),
+    ]
+    head_copy = pltpu.make_async_copy(head_i, rows(wfull, h_off, H), in_s.at[2])
+    for copy in sup_copies:
+        copy.start()
+
+    @pl.when(first)
+    def _():
+        head_copy.start()
+
+    @pl.when(core == 1)
+    def _():
+        pltpu.make_async_copy(head_t, rows(wfull, h_off, H), in_s.at[2]).start()
 
     greet(sib)
     for k in range(1, NZ):
@@ -90,11 +118,11 @@
         greet(plane(k, 0))
         greet(plane(k, 1))
 
-    h_off = pl.multiple_of(half * H, H)
-    wfull[pl.ds(h_off, H), :] = jnp.where(first, head_i[...], head_t[...])
+    for copy in sup_copies:
+        copy.wait()
     onehot = (lax.broadcasted_iota(jnp.int32, (S, N), 0) == sel[...]).astype(BF)
-    rows_i = dot(onehot, sup_i[...], ((0,), (0,))).astype(BF)
-    rows_t = dot(onehot, sup_t[...], ((0,), (0,))).astype(BF)
+    rows_i = dot(onehot, va[...], ((0,), (0,))).astype(BF)
+    rows_t = dot(onehot, vt[...], ((0,), (0,))).astype(BF)
     mine = pl.multiple_of(core * N, N)
     a[pl.ds(mine, N), :] = jnp.where(first, rows_i, rows_t)
     stage[...] = jnp.where(first, rows_t, rows_i)
@@ -106,6 +134,7 @@
         [jnp.broadcast_to(weight, (8, N)), jnp.zeros((8, N), F32)], axis=1
     )
 
+    head_copy.wait()
     pl.semaphore_wait(barrier, 1 + (NZ - 1) + 2 * (PLANE - 1))
 
     heads = []
@@ -148,25 +177,26 @@
     low = (column - high.astype(F32)).astype(BF)
     em[...] = jnp.concatenate([u.astype(BF), high, low, jnp.zeros((N2, EP - E - 2), BF)], axis=1)
 
-    line_order = (1, 7, 2, 6, 3, 5, 4)
-    plane_order = sorted(
-        range(1, PLANE),
-        key=lambda k: (min(k // 4, 4 - k // 4) + min(k % 4, 4 - k % 4), k),
-    )
+    line_order, plane_order = LINE[1:], SHEET[1:]
+
+    def img_at(k):
+        return LINE.index(k % NZ) * N2
+
+    def txt_at(k):
+        return SHEET.index(k) * N
 
     def ia(k):
         return remote(
-            em, rows(img, (NZ - k) % NZ * N2, N2), ia_s.at[k], ia_r.at[(NZ - k) % NZ], line(k)
-        )
-
-    def fwd(s):
-        block = rows(img, s * N2, N2)
-        src = em if s == 0 else block
-        return remote(src, block, if_s.at[s], ia_r.at[s], sib)
+            em, rows(img, img_at(-k), N2), ia_s.at[k], ia_r.at[(NZ - k) % NZ], line(k)
+        )
+
+    def fwd(k):
+        block = rows(img, img_at(k), N2)
+        return remote(em if k == 0 else block, block, if_s.at[k], ia_r.at[k], sib)
 
     def ta(k, c):
         return remote(
-            rows(em, c * N, N), rows(txt, back_slot(k) * N, N),
+            rows(em, c * N, N), rows(txt, txt_at(back_slot(k)), N),
             ta_s.at[2 * k + c], ta_r.at[back_slot(k)], plane(k, c),
         )
 
@@ -179,140 +209,131 @@
 
     @pl.when(core == 1)
     def _():
+        ta(0, 0).start()
         for k in plane_order:
             ta(k, 0).start()
             ta(k, 1).start()
-        ta(0, 0).start()
         txt[0:N, :] = em[N:N2, :]
 
     wo_copy = remote(wfull, wother, wo_s, wo_r, sib)
     wo_copy.start()
 
-    @pl.when(first)
-    def _():
-        arrived(rows(txt, 0, N), ta_r.at[0], ta_s.at[0])
-
-    for k in plane_order:
-        arrived(rows(txt, k * N, N), ta_r.at[k], ta_s.at[0])
-
     scale = lscale[0]
-    neg_scale, neg_bias = -lscale[0], -lbias[0]
-
-    def image_block(s):
-        block = img[pl.ds(pl.multiple_of(s * N2, N2), N2), :]
-        weight = block[:, E : E + 1].astype(F32) + block[:, E + 1 : E + 2].astype(F32)
-        e = jnp.exp(neg_scale * dot(block, txt[...], ((1,), (1,))) + neg_bias)
-        positive = weight / (1.0 + e)
-        return e, positive
-
-    def take(s):
+    neg_scale, neg_bias = -LOG2E * lscale[0], -LOG2E * lbias[0]
+
+    def take_image(k):
         @pl.when(first)
         def _():
-            if s:
-                arrived(rows(img, s * N2, N2), ia_r.at[s], ia_s.at[0])
-                fwd(s).start()
+            if k:
+                arrived(rows(img, img_at(k), N2), ia_r.at[k], ia_s.at[0])
+                fwd(k).start()
 
         @pl.when(core == 1)
         def _():
-            arrived(rows(img, s * N2, N2), ia_r.at[s], ia_s.at[0])
-
-    for s in (0,) + line_order:
-        take(s)
-        e, positive = image_block(s)
-        if s == 0:
-            r = lax.broadcasted_iota(jnp.int32, (N2, PLANE * N), 0)
-            c = lax.broadcasted_iota(jnp.int32, (N2, PLANE * N), 1)
-            same = (r == c + core * N) & (c < N)
-            positive = jnp.where(same, -positive * e, positive)
-        g[s * N2 : (s + 1) * N2, :] = positive.astype(BF)
-
-    def partial_i(s):
-        off = pl.multiple_of(s * N2, N2)
-        return dot(g[pl.ds(off, N2), :], txt[:, 0:E], ((1,), (0,)))
-
-    def pi(s):
-        return remote(rows(p_out, s * N2, N2), rows(p_in, s * N2, N2), pi_s.at[s], pi_r.at[s], sib)
+            arrived(rows(img, img_at(k), N2), ia_r.at[k], ia_s.at[0])
+
+    def take_text(k):
+        if k:
+            arrived(rows(txt, txt_at(k), N), ta_r.at[k], ta_s.at[0])
+        else:
+
+            @pl.when(first)
+            def _():
+                arrived(rows(txt, 0, N), ta_r.at[0], ta_s.at[0])
+
+    def tile(i, j, diagonal=False):
+        block = img[pl.ds(pl.multiple_of(i * B, B), B), :]
+        weight = block[:, E : E + 1].astype(F32) + block[:, E + 1 : E + 2].astype(F32)
+        other = txt[pl.ds(pl.multiple_of(j * B, B), B), :]
+        e = jnp.exp2(neg_scale * dot(block, other, ((1,), (1,))) + neg_bias)
+        value = weight / (1.0 + e)
+        if diagonal:
+            r = lax.broadcasted_iota(jnp.int32, (B, B), 0)
+            c = lax.broadcasted_iota(jnp.int32, (B, B), 1)
+            value = jnp.where((r == c + core * N) & (c < N), -value * e, value)
+        g[pl.ds(pl.multiple_of(i * B, B), B), pl.ds(pl.multiple_of(j * B, B), B)] = value.astype(BF)
+
+    for t in range(NZ * N2 // B):
+        for k in SHEET[4 * t : 4 * t + 4]:
+            take_text(k)
+        for k in LINE[2 * t : 2 * t + 2]:
+            take_image(k)
+        tile(t, t, t == 0)
+        if t:
+
+            @pl.loop(0, t)
+            def _(i, t=t):
+                tile(i, t)
+                tile(t, i)
+
+    def pi(k):
+        return remote(
+            rows(p_out, img_at(k), N2), rows(p_in, img_at(k), N2), pi_s.at[k], pi_r.at[k], sib
+        )
 
     def ri(k):
         return remote(
-            rows(p_out, k * N2, N2), rows(rs_i, (NZ - k) % NZ * N2, N2),
+            rows(p_out, img_at(k), N2), rows(rs_i, (NZ - k) % NZ * N2, N2),
             ri_s.at[k], ri_r.at[(NZ - k) % NZ], line(k),
         )
 
-    def wait_fwd(s):
-        fwd(s).wait_send()
+    def rt(k):
+        return remote(
+            rows(t_out, txt_at(k), N), rows(rs_t, (core * PLANE + back_slot(k)) * N, N),
+            rt_s.at[k], rt_r.at[core * PLANE + back_slot(k)], plane(k, 1),
+        )
+
+    def combine(k):
+        at = img_at(k)
+        arrived(rows(p_in, at, N2), pi_r.at[k], pi_s.at[k])
+        total = p_f[at : at + N2, :] + p_in[at : at + N2, :].astype(F32)
+        if k:
+            p_out[at : at + N2, :] = total.astype(BF)
+            ri(k).start()
+        else:
+            p_f[0:N2, :] = total
+
+    back_order = LINE[::-1]
+    for n in range(NZ + 1):
+        if n < NZ:
+            k = back_order[n]
+            at = img_at(k)
+            p_f[at : at + N2, :] = dot(g[at : at + N2, :], txt[:, 0:E], ((1,), (0,)))
+
+            @pl.when(core == 1)
+            def _(k=k, at=at):
+                p_out[at : at + N2, :] = p_f[at : at + N2, :].astype(BF)
+                pi(k).start()
+
+            b = NZ - 1 - n
+            block = dot(g[:, b * N2 : (b + 1) * N2], img[:, 0:E], ((0,), (0,)))
+            t_out[b * N2 : (b + 1) * N2, :] = block.astype(BF)
+            for k in SHEET[2 * b : 2 * b + 2]:
+                if k:
+                    rt(k).start()
+        if n:
+
+            @pl.when(first)
+            def _(n=n):
+                combine(back_order[n - 1])
 
     @pl.when(first)
     def _():
+        rt(0).start()
         for k in line_order:
-            ia(k).wait_send()
-        for s in range(NZ):
-            wait_fwd(s)
+            arrived(rows(rs_i, k * N2, N2), ri_r.at[k], ri_s.at[0])
+            p_f[0:N2, :] += rs_i[k * N2 : (k + 1) * N2, :].astype(F32)
 
     @pl.when(core == 1)
-    def _():
-        for k in plane_order:
-            ta(k, 0).wait_send()
-            ta(k, 1).wait_send()
-        ta(0, 0).wait_send()
-
-    send_order = line_order + (0,)
-    for s in send_order:
-        p_f[s * N2 : (s + 1) * N2, :] = partial_i(s)
-
-        @pl.when(core == 1)
-        def _(s=s):
-            p_out[s * N2 : (s + 1) * N2, :] = p_f[s * N2 : (s + 1) * N2, :].astype(BF)
-            pi(s).start()
-
-    @pl.when(first)
-    def _():
-        for s in send_order:
-            arrived(rows(p_in, s * N2, N2), pi_r.at[s], pi_s.at[s])
-            total = p_f[s * N2 : (s + 1) * N2, :] + p_in[s * N2 : (s + 1) * N2, :].astype(F32)
-            if s:
-                p_out[s * N2 : (s + 1) * N2, :] = total.astype(BF)
-                ri(s).start()
-            else:
-                p_f[0:N2, :] = total
-
-    def rt(k):
-        return remote(
-            rows(t_out, k * N, N), rows(rs_t, (core * PLANE + back_slot(k)) * N, N),
-            rt_s.at[k], rt_r.at[core * PLANE + back_slot(k)], plane(k, 1),
-        )
-
-    for b in range(PLANE // 2):
-        block = dot(g[:, b * N2 : (b + 1) * N2], img[:, 0:E], ((0,), (0,)))
-        t_out[b * N2 : (b + 1) * N2, :] = block.astype(BF)
-        for k in (2 * b, 2 * b + 1):
-            if k:
-                rt(k).start()
-            else:
-
-                @pl.when(first)
-                def _():
-                    rt(0).start()
-
-                @pl.when(core == 1)
-                def _(block=block):
-                    p_f[N : 2 * N, :] = block[0:N, :]
-
-    @pl.when(core == 1)
-    def _():
+    def _(block=block):
         arrived(rows(rs_t, 0, N), rt_r.at[0], rt_s.at[0])
         p_f[0:N, :] = rs_t[0:N, :].astype(F32)
+        p_f[N:N2, :] = block[0:N, :]
         for k in plane_order:
             for c in range(2):
                 at = c * PLANE + k
                 arrived(rows(rs_t, at * N, N), rt_r.at[at], rt_s.at[0])
                 p_f[c * N : (c + 1) * N, :] += rs_t[at * N : (at + 1) * N, :].astype(F32)
-
-    @pl.when(first)
-    def _():
-        for s in line_order:
-            arrived(rows(rs_i, s * N2, N2), ri_r.at[s], ri_s.at[0])
-            p_f[0:N2, :] += rs_i[s * N2 : (s + 1) * N2, :].astype(F32)
 
     grad = p_f[0:N2, :] * scale
     u = unit[...]
@@ -349,8 +370,12 @@
     gsv[core] = dot(moved, wfull[...], ((1,), (1,)))
     moved = dot(onehot, bo[...], ((1,), (0,))).astype(BF)
     gsv[1 - core] = dot(moved, wother[...], ((1,), (1,)))
-    gs_copy = pltpu.make_async_copy(gsv, gs, gs_s)
-    gs_copy.start()
+    gs_copies = [
+        pltpu.make_async_copy(gsv.at[0], gs_i, gs_s.at[0]),
+        pltpu.make_async_copy(gsv.at[1], gs_t, gs_s.at[1]),
+    ]
+    for copy in gs_copies:
+        copy.start()
 
     total = part(0)
     for k in plane_order:
@@ -434,13 +459,20 @@
     @pl.when(first)
     def _():
         for k in line_order:
+            ia(k).wait_send()
             ri(k).wait_send()
+        for k in LINE:
+            fwd(k).wait_send()
         rt(0).wait_send()
 
     @pl.when(core == 1)
     def _():
-        for s in range(NZ):
-            pi(s).wait_send()
+        for k in LINE:
+            pi(k).wait_send()
+        ta(0, 0).wait_send()
+        for k in plane_order:
+            ta(k, 0).wait_send()
+            ta(k, 1).wait_send()
 
     for k in plane_order:
         rt(k).wait_send()
@@ -461,7 +493,8 @@
     for k in [0] + mates:
         ad_copy(k).wait_send()
     own_copy.wait()
-    gs_copy.wait()
+    for copy in gs_copies:
+        copy.wait()
 
 
 def body(sup_i, sup_t, selected, buckets, weights, head_i, head_t, lscale, lbias, oscale):
@@ -474,7 +507,7 @@
 
     dma = pltpu.SemaphoreType.DMA
     buffers = [
-        space((N2, D)), space((N, D)), space((16, 128), F32), space((D, E)), space((D, E)),
+        space((S, D)), space((S, D)), space((N2, D)), space((N, D)), space((16, 128), F32), space((D, E)), space((D, E)),
         space((N2, E), F32), space((N2, 128), F32),
         space((N2, EP)), space((NZ * N2, EP)), space((PLANE * N, EP)),
         space((NZ * N2, PLANE * N)),
@@ -485,19 +518,20 @@
         space((PR, E)), space((16, E)),
     ]
     counts = [
-        2, 2, 0, 0, 0, 0, 0, 0,
+        3, 2, 2, 0, 0, 0, 0, 0, 0,
         NZ, NZ, NZ, 2 * PLANE, PLANE, NZ, NZ, NZ, NZ, PLANE, 2 * PLANE,
-        0, 0, 0, PLANE, PLANE, NZ, NZ, NZ, NZ, 0, PLANE, PLANE, PLANE, PLANE,
+        0, 0, 2, PLANE, PLANE, NZ, NZ, NZ, NZ, 0, PLANE, PLANE, PLANE, PLANE,
     ]
     sems = [dma((n,)) if n else dma for n in counts]
-    gs, gw = pl.pallas_call(
+    gs_i, gs_t, gw = pl.pallas_call(
         kernel,
         out_shape=(
-            jax.ShapeDtypeStruct((2, S, D), F32),
+            jax.ShapeDtypeStruct((S, D), F32),
+            jax.ShapeDtypeStruct((S, D), F32),
             jax.ShapeDtypeStruct((2, 8 * PR, E), BF),
         ),
-        in_specs=[vmem] * 4 + [smem] + [vmem] * 2 + [smem] * 3,
-        out_specs=(hbm, hbm),
+        in_specs=[hbm] * 2 + [vmem] * 2 + [smem] + [hbm] * 2 + [smem] * 3,
+        out_specs=(hbm, hbm, hbm),
         scratch_shapes=buffers + sems,
         compiler_params=pltpu.CompilerParams(
             collective_id=0, has_side_effects=True, vmem_limit_bytes=56 * 1024 * 1024
@@ -507,7 +541,7 @@
         head_i, head_t, lscale, lbias, oscale,
     )
     gw = gw.reshape(2, 8, PR, E)[:, :, 0:PIECE, :].reshape(2, H, E).astype(F32)
-    return gw[0], gw[1], gs[0], gs[1]
+    return gw[0], gw[1], gs_i, gs_t
 
 
 def solution(mesh):

time: 129 us -> 123 us (0.953)
  Pallas kernels: 119 us -> 113 us
    pallas_call x1, Pallas kernels: 119 us -> 113 us  [body(): pl.pallas_call(kernel, out_shape=(jax.ShapeDtypeStruct((S, D), F32), jax....]
    unnamed x2 -> x6, local copies, waits for them, and re-layouts: 1.1 us -> 3.16 us
    squeeze x1 -> x0, local copies, waits for them, and re-layouts: 1.78 us -> none  [body(): return (gw[0], gw[1], gs[0], gs[1])]
where the time goes in v2:
time: 123 us; the launch traced here: 122 us
  Pallas kernels  113 us (92%)
  local copies, waits for them, and re-layouts  4.95 us (4%)
  between operations  2.59 us (2%)
  other arithmetic  1.57 us (1%)
    pallas_call x1, Pallas kernels, body(): pl.pallas_call(kernel, out_shape=(jax.ShapeDtypeStruct((S, D), F32), jax....  113 us
    unnamed x6, local copies, waits for them, and re-layouts  3.16 us

profile of v2, /device:TPU:35, one launch (start us, length us, event | category | flops | bytes accessed | tf_op | source)
XLA Modules:
  0.0 121.9 jit_solution(7071695409628330374)
XLA Ops:
  2.6 112.8 %shard_map.129 = (f32[320,1152]{1,0:T(8,128)}, f32[320,1152]{1,0:T(8,128)}, bf16[2,640,576]{2,1,0:T(8,128)(2,1)}) custom-call(bf16[320,1152]{1,0:T(8,128)(2,1)} %sup_i.1, bf16[320,1152]{1,0:T(8,128)(2,1)} %sup_t.1, s32[1,64]{1,0:T(1,128)} %bitcast.8, s32[1,64]{1,0:T(1,128)} %bitcast.9, f32[16]{0:T(128)} %wts.1, bf16[576,576]{1,0:T(8,128)(2,1)} %head_i.1, ...), custom_call_target="tpu_custom_call" | custom-call | tf_op jit(solution)/shard_map/pallas_call | solution.py:526
  115.3 1.6 %slice_convert_fusion = f32[2,8,72,576]{3,2,1,0:T(8,128)S(1)} fusion(bf16[2,8,80,576]{3,2,1,0:T(8,128)(2,1)} %bitcast.7), kind=kLoop, calls=%fused_computation | loop fusion | flops 663552 | bytes 3981312 | tf_op jit(solution)/shard_map/convert_element_type | solution.py:543
  116.9 0.0 copy-start.1
  116.9 1.8 %fusion = (f32[1,8,72,576]{3,2,1,0:T(8,128)}, f32[1,8,72,576]{3,2,1,0:T(8,128)}) fusion(f32[2,8,72,576]{3,2,1,0:T(8,128)S(1)} %slice_convert_fusion), kind=kLoop, calls=%fused_computation.1 | loop fusion | bytes 5308416 | tf_op jit(solution)/shard_map/slice | solution.py:544
  118.7 0.1 copy-done.1
  118.9 0.0 copy-start
  118.9 1.1 copy.19
  120.0 0.8 copy-done
  120.8 1.1 copy.20
Async XLA Ops:
  116.9 1.9 %copy-start.1 = (f32[320,1152]{1,0:T(8,128)S(1)}, f32[320,1152]{1,0:T(8,128)}, u32[]{:S(2)}) copy-start(f32[320,1152]{1,0:T(8,128)} %get-tuple-element.18) | copy-start | bytes 4423684
  118.9 1.9 %copy-start = (f32[320,1152]{1,0:T(8,128)S(1)}, f32[320,1152]{1,0:T(8,128)}, u32[]{:S(2)}) copy-start(f32[320,1152]{1,0:T(8,128)} %get-tuple-element.19) | copy-start | bytes 4423684

commit v3 on v2

--- a/solution.py
+++ b/solution.py
@@ -20,9 +20,9 @@
 H = D // 2
 E = 576
 EP = 640
-PIECE = D // PLANE
+PIECE = 48
+Z_ROWS = PIECE * NZ // 2
 B = 256
-PR = 80
 NB = 16
 LOG2E = 1.4426950408889634
 
@@ -61,10 +61,11 @@
     gs_i, gs_t, gw,
     va, vt, a, stage, cbuf, wfull, wother, unit, length,
     em, img, txt, g, p_f, p_out, p_in, t_out, rs_i, rs_t,
-    bk, bo, gsv, dwf, dws, r1, psum, r2, fin, res,
+    bk, bo, gsv, dwf, dws, dwz, r1, rz, r3, zsum, zfin, psum, r2, fin, res,
     in_s, w_s, w_r, rows_s, rows_r, c_s, c_r, wo_s, wo_r,
     ia_s, ia_r, if_s, ta_s, ta_r, pi_s, pi_r, ri_s, ri_r, rt_s, rt_r,
-    bk_s, bk_r, gs_s, r1_s, r1_r, r2_s, r2_r, f_s, f_r, own_s, ag_s, ag_r, ad_s, ad_r,
+    bk_s, bk_r, gs_s, r1_s, r1_r, rz_s, rz_r, r3_s, r3_r, r2_s, r2_r, f_s, f_r,
+    zg_s, zg_r, zd_s, zd_r, own_s, ag_s, ag_r, ad_s, ad_r,
 ):
     x, y, z, core = place()
     half = lax.rem(x, 2)
@@ -128,8 +129,8 @@
     stage[...] = jnp.where(first, rows_t, rows_i)
     weight = jnp.zeros((1, N), F32)
     for n in range(NB):
-        weight = jnp.where(bkt[...] == n, wts[n], weight)
-    weight = oscale[0] * weight / PAIRS
+        weight = jnp.where(bkt[...] == n, wts[:, n : n + 1], weight)
+    weight = oscale[...] * weight / PAIRS
     cbuf[pl.ds(pl.multiple_of(core * 8, 8), 8), :] = jnp.concatenate(
         [jnp.broadcast_to(weight, (8, N)), jnp.zeros((8, N), F32)], axis=1
     )
@@ -218,8 +219,8 @@
     wo_copy = remote(wfull, wother, wo_s, wo_r, sib)
     wo_copy.start()
 
-    scale = lscale[0]
-    neg_scale, neg_bias = -LOG2E * lscale[0], -LOG2E * lbias[0]
+    scale = lscale[...]
+    neg_scale, neg_bias = -LOG2E * lscale[...], -LOG2E * lbias[...]
 
     def take_image(k):
         @pl.when(first)
@@ -344,23 +345,39 @@
 
     dwf[...] = dot(a[...], back, ((0,), (0,)))
 
-    def piece(px, py):
-        return (lax.rem(px, 2) * 2 + lax.div(px, 2)) * NY + py
+    def z_row(k):
+        at = lax.rem(z + k, NZ)
+        return lax.div(at, NZ // 2), lax.rem(at, NZ // 2) * PIECE
+
+    def p_row(k):
+        px, py = lax.rem(x + k // NY, NX), lax.rem(y + k % NY, NY)
+        return lax.rem(px, 2), Z_ROWS + (lax.div(px, 2) * NY + py) * PIECE
+
+    def part(where):
+        which, row = where
+        return dwf[pl.ds(pl.multiple_of(which * H + row, PIECE), PIECE), :]
+
+    def block(ref, k):
+        return rows(ref, k * PIECE, PIECE)
 
     def r1_copy(k):
         return remote(
-            rows(dws, k * PR, PR), rows(r1, back_slot(k) * PR, PR),
-            r1_s.at[k], r1_r.at[back_slot(k)], plane(k),
-        )
-
-    def part(k):
-        q = piece(lax.rem(x + k // NY, NX), lax.rem(y + k % NY, NY))
-        return dwf[pl.ds(pl.multiple_of(q * PIECE, 8), PIECE), :]
-
-    for k in plane_order:
-        dws[k * PR : (k + 1) * PR, :] = jnp.concatenate(
-            [part(k), jnp.zeros((PR - PIECE, E), F32)], axis=0
-        ).astype(BF)
+            block(dws, k), block(r1, back_slot(k)), r1_s.at[k], r1_r.at[back_slot(k)], plane(k)
+        )
+
+    def rz_copy(k):
+        back_k = (NZ - k) % NZ
+        return remote(block(dwz, k), block(rz, back_k), rz_s.at[k], rz_r.at[back_k], line(k))
+
+    def fill(ref, k, where):
+        ref[k * PIECE : (k + 1) * PIECE, :] = part(where).astype(BF)
+
+    for n, k in enumerate(plane_order[::-1]):
+        if n % 2 == 0 and n // 2 < NZ - 1:
+            kz = line_order[::-1][n // 2]
+            fill(dwz, kz, z_row(kz))
+            rz_copy(kz).start()
+        fill(dws, k, p_row(k))
         r1_copy(k).start()
 
     arrived(bo, bk_r, bk_s)
@@ -377,81 +394,139 @@
     for copy in gs_copies:
         copy.start()
 
-    total = part(0)
+    z_half, z_at = z_row(0)
+    holder = half == z_half
+    total = part((z_half, z_at))
+    for k in line_order:
+        arrived(block(rz, k), rz_r.at[k], rz_s.at[k])
+        total += rz[k * PIECE : (k + 1) * PIECE, :].astype(F32)
+    zsum[...] = total.astype(BF)
+
+    def wants(k):
+        return lax.rem(x + k // NY, 2) == z_half
+
+    def r3_copy(k):
+        return remote(zsum, block(r3, back_slot(k)), r3_s.at[k], r3_r.at[back_slot(k)], plane(k))
+
     for k in plane_order:
-        arrived(rows(r1, k * PR, PR), r1_r.at[k], r1_s.at[k])
-        total += r1[k * PR : (k + 1) * PR, :].astype(F32)[0:PIECE, :]
-    whole = jnp.concatenate([total, jnp.zeros((PR - PIECE, E), F32)], axis=0)
-    psum[...] = whole.astype(BF)
-
+
+        @pl.when(wants(k))
+        def _(k=k):
+            r3_copy(k).start()
+
+    dwf[0:PIECE, :] = total
+
+    total = part(p_row(0))
+    for k in plane_order:
+        arrived(block(r1, k), r1_r.at[k], r1_s.at[k])
+        total += r1[k * PIECE : (k + 1) * PIECE, :].astype(F32)
+    psum[...] = total.astype(BF)
     rank = lax.rem(z + 4 * core, NZ)
 
     def rank_of(k):
         return lax.rem(rank + k, NZ)
 
-    def tile(ref, at, base=0):
-        return rows(ref, pl.multiple_of(base + at * 16, 16), 16)
+    def sums(k):
+        return lax.rem(rank_of(k), 3) == 0
+
+    def tile_at(k):
+        return pl.multiple_of(lax.div(rank_of(k), 3) * 16, 16)
 
     def r2_copy(k):
         back_k = (NZ - k) % NZ
         return remote(
-            tile(psum, rank_of(k)), rows(r2, back_k * 16, 16), r2_s.at[k], r2_r.at[back_k], line(k)
+            rows(psum, tile_at(k), 16), rows(r2, back_k * 16, 16),
+            r2_s.at[k], r2_r.at[back_k], line(k),
         )
 
     for k in line_order:
 
-        @pl.when(rank_of(k) < 5)
+        @pl.when(sums(k))
         def _(k=k):
             r2_copy(k).start()
 
     def f_copy(k):
-        return remote(res, tile(fin, rank), f_s.at[k], f_r.at[(NZ - k) % NZ], line(k))
-
-    @pl.when(rank < 5)
-    def _():
-        total = psum[pl.ds(pl.multiple_of(rank * 16, 16), 16), :].astype(F32)
+        return remote(res, rows(fin, tile_at(0), 16), f_s.at[k], f_r.at[(NZ - k) % NZ], line(k))
+
+    @pl.when(sums(0))
+    def _():
+        total = psum[pl.ds(tile_at(0), 16), :].astype(F32)
         for k in line_order:
             arrived(rows(r2, k * 16, 16), r2_r.at[k], r2_s.at[k])
             total += r2[k * 16 : (k + 1) * 16, :].astype(F32)
         res[...] = total.astype(BF)
         for k in line_order:
             f_copy(k).start()
-        fin[pl.ds(pl.multiple_of(rank * 16, 16), 16), :] = total.astype(BF)
+        fin[pl.ds(tile_at(0), 16), :] = total.astype(BF)
+
+    def shelf(modality, row):
+        return gw.at[modality, pl.ds(pl.multiple_of(row, PIECE), PIECE), :]
+
+    def zg_copy(k):
+        return remote(
+            zfin, shelf(core, z_row(0)[1]), zg_s.at[k], zg_r.at[(NZ - k) % NZ], line(k)
+        )
+
+    def zd_copy(k, modality=core):
+        to = shelf(modality, z_row(k)[1])
+        return remote(zfin if k == 0 else to, to, zd_s.at[k], zd_r.at[k], sib)
+
+    def holds(k):
+        return z_row(k)[0] == half
+
+    own_z = pltpu.make_async_copy(zfin, shelf(core, z_row(0)[1]), own_s.at[0])
+
+    @pl.when(holder)
+    def _():
+        for k in plane_order:
+            arrived(block(r3, k), r3_r.at[k], r3_s.at[k])
+            dwf[0:PIECE, :] += r3[k * PIECE : (k + 1) * PIECE, :].astype(F32)
+        zfin[...] = dwf[0:PIECE, :].astype(BF)
+        for k in line_order:
+            zg_copy(k).start()
+        zd_copy(0).start()
+        own_z.start()
 
     for k in line_order:
 
-        @pl.when(rank_of(k) < 5)
-        def _(k=k):
-            arrived(tile(fin, rank_of(k)), f_r.at[k], f_s.at[k])
-
-    def held(px, py):
-        return pl.multiple_of((lax.div(px, 2) * NY + py) * PR, PR)
+        @pl.when(sums(k))
+        def _(k=k):
+            arrived(rows(fin, tile_at(k), 16), f_r.at[k], f_s.at[k])
 
     mates = [k for k in plane_order if (k // NY) % 2 == 0]
 
-    def mate(k):
-        return lax.rem(x + k // NY, NX), lax.rem(y + k % NY, NY)
-
     def ag_copy(k):
         return remote(
-            fin, gw.at[core, pl.ds(held(x, y), PR), :],
-            ag_s.at[k], ag_r.at[back_slot(k)], plane(k),
-        )
-
-    def ad_copy(k):
-        block = gw.at[core, pl.ds(held(*mate(k)), PR), :]
-        return remote(fin if k == 0 else block, block, ad_s.at[k], ad_r.at[k], sib)
+            fin, shelf(core, p_row(0)[1]), ag_s.at[k], ag_r.at[back_slot(k)], plane(k)
+        )
+
+    def ad_copy(k, modality=core):
+        to = shelf(modality, p_row(k)[1])
+        return remote(fin if k == 0 else to, to, ad_s.at[k], ad_r.at[k], sib)
 
     for k in mates:
         ag_copy(k).start()
     ad_copy(0).start()
-    own_copy = pltpu.make_async_copy(fin, gw.at[core, pl.ds(held(x, y), PR), :], own_s)
-    own_copy.start()
+    own_p = pltpu.make_async_copy(fin, shelf(core, p_row(0)[1]), own_s.at[1])
+    own_p.start()
+    for k in line_order:
+
+        @pl.when(holds(k))
+        def _(k=k):
+            arrived(shelf(core, z_row(k)[1]), zg_r.at[k], zg_s.at[k])
+            zd_copy(k).start()
+
     for k in mates:
-        arrived(gw.at[core, pl.ds(held(*mate(k)), PR), :], ag_r.at[k], ag_s.at[k])
+        arrived(shelf(core, p_row(k)[1]), ag_r.at[k], ag_s.at[k])
         ad_copy(k).start()
+    for k in LINE:
+
+        @pl.when(holds(k))
+        def _(k=k):
+            arrived(shelf(1 - core, z_row(k)[1]), zd_r.at[k], zd_s.at[k])
+
     for k in [0] + mates:
-        arrived(gw.at[1 - core, pl.ds(held(*mate(k)), PR), :], ad_r.at[k], ad_s.at[k])
+        arrived(shelf(1 - core, p_row(k)[1]), ad_r.at[k], ad_s.at[k])
 
     for copy in heads + [rows_copy, c_copy, wo_copy, bk_copy]:
         copy.wait_send()
@@ -478,28 +553,67 @@
         rt(k).wait_send()
         r1_copy(k).wait_send()
     for k in line_order:
-
-        @pl.when(rank_of(k) < 5)
+        rz_copy(k).wait_send()
+
+        @pl.when(sums(k))
         def _(k=k):
             r2_copy(k).wait_send()
 
-    @pl.when(rank < 5)
+    for k in plane_order:
+
+        @pl.when(wants(k))
+        def _(k=k):
+            r3_copy(k).wait_send()
+
+    @pl.when(sums(0))
     def _():
         for k in line_order:
             f_copy(k).wait_send()
+
+    @pl.when(holder)
+    def _():
+        for k in line_order:
+            zg_copy(k).wait_send()
+        own_z.wait()
+
+    for k in LINE:
+
+        @pl.when(holds(k))
+        def _(k=k):
+            zd_copy(k).wait_send()
 
     for k in mates:
         ag_copy(k).wait_send()
     for k in [0] + mates:
         ad_copy(k).wait_send()
-    own_copy.wait()
+    own_p.wait()
     for copy in gs_copies:
         copy.wait()
 
 
+def finish(gw, gs_i, gs_t, out_hi, out_ht, out_i, out_t, narrow, wide, in_s, out_s, gs_s):
+    loads = [pltpu.make_async_copy(gw.at[m], narrow.at[m], in_s.at[m]) for m in range(2)]
+    for copy in loads:
+        copy.start()
+    step = S // 4
+    copies = []
+    for m, (src, dst) in enumerate(((gs_i, out_i), (gs_t, out_t))):
+        for n in range(4):
+            at = pl.ds(n * step, step)
+            copies.append(pltpu.make_async_copy(src.at[at, :], dst.at[at, :], gs_s.at[4 * m + n]))
+    for copy in copies:
+        copy.start()
+    for m, dst in enumerate((out_hi, out_ht)):
+        loads[m].wait()
+        wide[m] = narrow[m].astype(F32)
+        copies.append(pltpu.make_async_copy(wide.at[m], dst, out_s.at[m]))
+        copies[-1].start()
+    for copy in copies:
+        copy.wait()
+
+
 def body(sup_i, sup_t, selected, buckets, weights, head_i, head_t, lscale, lbias, oscale):
     vmem = pl.BlockSpec(memory_space=pltpu.VMEM)
-    smem = pl.BlockSpec(memory_space=pltpu.SMEM)
     hbm = pl.BlockSpec(memory_space=pl.ANY)
 
     def space(shape, dtype=BF):
@@ -507,20 +621,23 @@
 
     dma = pltpu.SemaphoreType.DMA
     buffers = [
-        space((S, D)), space((S, D)), space((N2, D)), space((N, D)), space((16, 128), F32), space((D, E)), space((D, E)),
+        space((S, D)), space((S, D)), space((N2, D)), space((N, D)), space((16, 128), F32),
+        space((D, E)), space((D, E)),
         space((N2, E), F32), space((N2, 128), F32),
         space((N2, EP)), space((NZ * N2, EP)), space((PLANE * N, EP)),
         space((NZ * N2, PLANE * N)),
         space((NZ * N2, E), F32), space((NZ * N2, E)), space((NZ * N2, E)), space((PLANE * N, E)),
         space((NZ * N2, E)), space((2 * PLANE * N, E)),
         space((N2, E)), space((N, E)), space((2, S, D), F32), space((D, E), F32),
-        space((PLANE * PR, E)), space((PLANE * PR, E)), space((PR, E)), space((NZ * 16, E)),
-        space((PR, E)), space((16, E)),
+        space((PLANE * PIECE, E)), space((NZ * PIECE, E)), space((PLANE * PIECE, E)),
+        space((NZ * PIECE, E)), space((PLANE * PIECE, E)), space((PIECE, E)), space((PIECE, E)),
+        space((PIECE, E)), space((NZ * 16, E)), space((PIECE, E)), space((16, E)),
     ]
     counts = [
         3, 2, 2, 0, 0, 0, 0, 0, 0,
         NZ, NZ, NZ, 2 * PLANE, PLANE, NZ, NZ, NZ, NZ, PLANE, 2 * PLANE,
-        0, 0, 2, PLANE, PLANE, NZ, NZ, NZ, NZ, 0, PLANE, PLANE, PLANE, PLANE,
+        0, 0, 2, PLANE, PLANE, NZ, NZ, PLANE, PLANE, NZ, NZ, NZ, NZ,
+        NZ, NZ, NZ, NZ, 2, PLANE, PLANE, PLANE, PLANE,
     ]
     sems = [dma((n,)) if n else dma for n in counts]
     gs_i, gs_t, gw = pl.pallas_call(
@@ -528,20 +645,25 @@
         out_shape=(
             jax.ShapeDtypeStruct((S, D), F32),
             jax.ShapeDtypeStruct((S, D), F32),
-            jax.ShapeDtypeStruct((2, 8 * PR, E), BF),
+            jax.ShapeDtypeStruct((2, H, E), BF),
         ),
-        in_specs=[hbm] * 2 + [vmem] * 2 + [smem] + [hbm] * 2 + [smem] * 3,
+        in_specs=[hbm] * 2 + [vmem] * 3 + [hbm] * 2 + [vmem] * 3,
         out_specs=(hbm, hbm, hbm),
         scratch_shapes=buffers + sems,
         compiler_params=pltpu.CompilerParams(
             collective_id=0, has_side_effects=True, vmem_limit_bytes=56 * 1024 * 1024
         ),
     )(
-        sup_i, sup_t, selected.reshape(1, N), buckets.reshape(1, N), weights,
-        head_i, head_t, lscale, lbias, oscale,
+        sup_i, sup_t, selected.reshape(1, N), buckets.reshape(1, N), weights.reshape(1, NB),
+        head_i, head_t, lscale.reshape(1, 1), lbias.reshape(1, 1), oscale.reshape(1, 1),
     )
-    gw = gw.reshape(2, 8, PR, E)[:, :, 0:PIECE, :].reshape(2, H, E).astype(F32)
-    return gw[0], gw[1], gs_i, gs_t
+    return pl.pallas_call(
+        finish,
+        out_shape=(jax.ShapeDtypeStruct((H, E), F32),) * 2 + (jax.ShapeDtypeStruct((S, D), F32),) * 2,
+        in_specs=[hbm] * 3,
+        out_specs=(hbm,) * 4,
+        scratch_shapes=[space((2, H, E)), space((2, H, E), F32), dma((2,)), dma((2,)), dma((8,))],
+    )(gw, gs_i, gs_t)
 
 
 def solution(mesh):

time: 123 us -> 202 us (1.64)
  Pallas kernels: 113 us -> 199 us
  local copies, waits for them, and re-layouts: 4.95 us -> 0 us
    pallas_call x0 -> x1, Pallas kernels: none -> 90.6 us  [body(): pl.pallas_call(finish, out_shape=(jax.ShapeDtypeStruct((H, E), F32),) * 2...]
    pallas_call x1, Pallas kernels: 113 us -> 108 us  [body(): pl.pallas_call(kernel, out_shape=(jax.ShapeDtypeStruct((S, D), F32), jax....]
    unnamed x6 -> x0, local copies, waits for them, and re-layouts: 3.16 us -> none
where the time goes in v3:
time: 202 us; the launch traced here: 201 us
  Pallas kernels  199 us (99%)
  between operations  2.58 us (1%)
    pallas_call x1, Pallas kernels, body(): pl.pallas_call(kernel, out_shape=(jax.ShapeDtypeStruct((S, D), F32), jax....  108 us
    pallas_call x1, Pallas kernels, body(): pl.pallas_call(finish, out_shape=(jax.ShapeDtypeStruct((H, E), F32),) * 2...  90.6 us

profile of v3, /device:TPU:35, one launch (start us, length us, event | category | flops | bytes accessed | tf_op | source)
XLA Modules:
  0.0 201.3 jit_solution(16912602474488766439)
XLA Ops:
  2.6 108.2 %shard_map.129 = (f32[320,1152]{1,0:T(8,128)}, f32[320,1152]{1,0:T(8,128)}, bf16[2,576,576]{2,1,0:T(8,128)(2,1)}) custom-call(bf16[320,1152]{1,0:T(8,128)(2,1)} %sup_i.1, bf16[320,1152]{1,0:T(8,128)(2,1)} %sup_t.1, s32[1,64]{1,0:T(1,128)} %bitcast.9, s32[1,64]{1,0:T(1,128)} %bitcast.10, f32[1,16]{1,0:T(1,128)} %bitcast.11, bf16[576,576]{1,0:T(8,128)(2,1)} %head_i.1, ...), custom_call_target="tpu_custom_call" | custom-call | tf_op jit(solution)/shard_map/pallas_call | solution.py:643
  110.8 90.6 %shard_map.130 = (f32[576,576]{1,0:T(8,128)}, f32[576,576]{1,0:T(8,128)}, f32[320,1152]{1,0:T(8,128)}, f32[320,1152]{1,0:T(8,128)}) custom-call(bf16[2,576,576]{2,1,0:T(8,128)(2,1)} %get-tuple-element.7.gw, f32[320,1152]{1,0:T(8,128)} %get-tuple-element.8.gs_i, f32[320,1152]{1,0:T(8,128)} %get-tuple-element.9.gs_t), custom_call_target="tpu_custom_call" | custom-call | tf_op jit(solution)/shard_map/pallas_call | solution.py:660

commit v4 on v3

--- a/solution.py
+++ b/solution.py
@@ -21,6 +21,7 @@
 E = 576
 EP = 640
 PIECE = 48
+TILES = 16
 Z_ROWS = PIECE * NZ // 2
 B = 256
 NB = 16
@@ -61,11 +62,11 @@
     gs_i, gs_t, gw,
     va, vt, a, stage, cbuf, wfull, wother, unit, length,
     em, img, txt, g, p_f, p_out, p_in, t_out, rs_i, rs_t,
-    bk, bo, gsv, dwf, dws, dwz, r1, rz, r3, zsum, zfin, psum, r2, fin, res,
+    bk, bo, gsv, dwf, dws, dwz, r1, rz, r3, zsum, zres, zft, zfin, psum, r2, res, fint, fin, gwv,
     in_s, w_s, w_r, rows_s, rows_r, c_s, c_r, wo_s, wo_r,
     ia_s, ia_r, if_s, ta_s, ta_r, pi_s, pi_r, ri_s, ri_r, rt_s, rt_r,
-    bk_s, bk_r, gs_s, r1_s, r1_r, rz_s, rz_r, r3_s, r3_r, r2_s, r2_r, f_s, f_r,
-    zg_s, zg_r, zd_s, zd_r, own_s, ag_s, ag_r, ad_s, ad_r,
+    bk_s, bk_r, gs_s, r1_s, r1_r, rz_s, rz_r, r3_s, r3_r, e3_s, e3_r, r2_s, r2_r, f_s, f_r,
+    zg_s, zg_r, zd_s, zd_r, own_s, gw_s, ag_s, ag_r, ad_s, ad_r,
 ):
     x, y, z, core = place()
     half = lax.rem(x, 2)
@@ -396,71 +397,94 @@
 
     z_half, z_at = z_row(0)
     holder = half == z_half
+
+    def to_tiles(ref, value):
+        for t in range(TILES):
+            r, c = 16 * (t // 5), 128 * (t % 5)
+            if t == TILES - 1:
+                piece = jnp.zeros((16, 128), F32)
+            elif c + 128 > E:
+                piece = jnp.concatenate([value[r : r + 16, c:E], jnp.zeros((16, c + 128 - E), F32)], axis=1)
+            else:
+                piece = value[r : r + 16, c : c + 128]
+            ref[16 * t : 16 * t + 16, :] = piece.astype(BF)
+
+    def from_tiles(ref):
+        bands = []
+        for r in range(3):
+            tiles = [ref[16 * (5 * r + c) : 16 * (5 * r + c) + 16, :] for c in range(5)]
+            bands.append(jnp.concatenate(tiles, axis=1)[:, 0:E])
+        return jnp.concatenate(bands, axis=0)
+
     total = part((z_half, z_at))
     for k in line_order:
         arrived(block(rz, k), rz_r.at[k], rz_s.at[k])
         total += rz[k * PIECE : (k + 1) * PIECE, :].astype(F32)
-    zsum[...] = total.astype(BF)
+    to_tiles(zsum, total)
+
+    def p_tile(k):
+        return pl.multiple_of((lax.rem(x + k // NY, NX) * NY + lax.rem(y + k % NY, NY)) * 16, 16)
+
+    def r3_copy(k):
+        return remote(
+            rows(zsum, p_tile(k), 16), rows(r3, back_slot(k) * 16, 16),
+            r3_s.at[k], r3_r.at[back_slot(k)], plane(k),
+        )
+
+    for k in plane_order[::-1]:
+        r3_copy(k).start()
+
+    total = part(p_row(0))
+    for k in plane_order[::-1]:
+        arrived(block(r1, k), r1_r.at[k], r1_s.at[k])
+        total += r1[k * PIECE : (k + 1) * PIECE, :].astype(F32)
+    to_tiles(psum, total)
+
+    def l_tile(k):
+        return pl.multiple_of(lax.rem(z + k, NZ) * 32, 32)
+
+    def r2_copy(k):
+        back_k = (NZ - k) % NZ
+        return remote(
+            rows(psum, l_tile(k), 32), rows(r2, back_k * 32, 32), r2_s.at[k], r2_r.at[back_k], line(k)
+        )
+
+    for k in line_order[::-1]:
+        r2_copy(k).start()
 
     def wants(k):
         return lax.rem(x + k // NY, 2) == z_half
 
-    def r3_copy(k):
-        return remote(zsum, block(r3, back_slot(k)), r3_s.at[k], r3_r.at[back_slot(k)], plane(k))
-
+    def e3_copy(k):
+        return remote(zres, rows(zft, p_tile(0), 16), e3_s.at[k], e3_r.at[back_slot(k)], plane(k))
+
+    total = zsum[pl.ds(p_tile(0), 16), :].astype(F32)
     for k in plane_order:
+        arrived(rows(r3, k * 16, 16), r3_r.at[k], r3_s.at[k])
+        total += r3[k * 16 : (k + 1) * 16, :].astype(F32)
+    zres[...] = total.astype(BF)
+    for k in plane_order[::-1]:
 
         @pl.when(wants(k))
         def _(k=k):
-            r3_copy(k).start()
-
-    dwf[0:PIECE, :] = total
-
-    total = part(p_row(0))
-    for k in plane_order:
-        arrived(block(r1, k), r1_r.at[k], r1_s.at[k])
-        total += r1[k * PIECE : (k + 1) * PIECE, :].astype(F32)
-    psum[...] = total.astype(BF)
-    rank = lax.rem(z + 4 * core, NZ)
-
-    def rank_of(k):
-        return lax.rem(rank + k, NZ)
-
-    def sums(k):
-        return lax.rem(rank_of(k), 3) == 0
-
-    def tile_at(k):
-        return pl.multiple_of(lax.div(rank_of(k), 3) * 16, 16)
-
-    def r2_copy(k):
-        back_k = (NZ - k) % NZ
-        return remote(
-            rows(psum, tile_at(k), 16), rows(r2, back_k * 16, 16),
-            r2_s.at[k], r2_r.at[back_k], line(k),
-        )
-
+            e3_copy(k).start()
+
+    zft[pl.ds(p_tile(0), 16), :] = total.astype(BF)
+
+    def f_copy(k):
+        return remote(res, rows(fint, l_tile(0), 32), f_s.at[k], f_r.at[(NZ - k) % NZ], line(k))
+
+    total = psum[pl.ds(l_tile(0), 32), :].astype(F32)
     for k in line_order:
-
-        @pl.when(sums(k))
-        def _(k=k):
-            r2_copy(k).start()
-
-    def f_copy(k):
-        return remote(res, rows(fin, tile_at(0), 16), f_s.at[k], f_r.at[(NZ - k) % NZ], line(k))
-
-    @pl.when(sums(0))
-    def _():
-        total = psum[pl.ds(tile_at(0), 16), :].astype(F32)
-        for k in line_order:
-            arrived(rows(r2, k * 16, 16), r2_r.at[k], r2_s.at[k])
-            total += r2[k * 16 : (k + 1) * 16, :].astype(F32)
-        res[...] = total.astype(BF)
-        for k in line_order:
-            f_copy(k).start()
-        fin[pl.ds(tile_at(0), 16), :] = total.astype(BF)
+        arrived(rows(r2, k * 32, 32), r2_r.at[k], r2_s.at[k])
+        total += r2[k * 32 : (k + 1) * 32, :].astype(F32)
+    res[...] = total.astype(BF)
+    for k in line_order[::-1]:
+        f_copy(k).start()
+    fint[pl.ds(l_tile(0), 32), :] = total.astype(BF)
 
     def shelf(modality, row):
-        return gw.at[modality, pl.ds(pl.multiple_of(row, PIECE), PIECE), :]
+        return gwv.at[modality, pl.ds(pl.multiple_of(row, PIECE), PIECE), :]
 
     def zg_copy(k):
         return remote(
@@ -479,19 +503,16 @@
     @pl.when(holder)
     def _():
         for k in plane_order:
-            arrived(block(r3, k), r3_r.at[k], r3_s.at[k])
-            dwf[0:PIECE, :] += r3[k * PIECE : (k + 1) * PIECE, :].astype(F32)
-        zfin[...] = dwf[0:PIECE, :].astype(BF)
+            arrived(rows(zft, p_tile(k), 16), e3_r.at[k], e3_s.at[k])
+        zfin[...] = from_tiles(zft)
         for k in line_order:
             zg_copy(k).start()
         zd_copy(0).start()
         own_z.start()
 
     for k in line_order:
-
-        @pl.when(sums(k))
-        def _(k=k):
-            arrived(rows(fin, tile_at(k), 16), f_r.at[k], f_s.at[k])
+        arrived(rows(fint, l_tile(k), 32), f_r.at[k], f_s.at[k])
+    fin[...] = from_tiles(fint)
 
     mates = [k for k in plane_order if (k // NY) % 2 == 0]
 
@@ -519,6 +540,15 @@
     for k in mates:
         arrived(shelf(core, p_row(k)[1]), ag_r.at[k], ag_s.at[k])
         ad_copy(k).start()
+    @pl.when(holder)
+    def _():
+        own_z.wait()
+
+    own_p.wait()
+    gw_copies = [
+        pltpu.make_async_copy(gwv.at[m], gw.at[m], gw_s.at[n]) for n, m in enumerate((core, 1 - core))
+    ]
+    gw_copies[0].start()
     for k in LINE:
 
         @pl.when(holds(k))
@@ -527,6 +557,7 @@
 
     for k in [0] + mates:
         arrived(shelf(1 - core, p_row(k)[1]), ad_r.at[k], ad_s.at[k])
+    gw_copies[1].start()
 
     for copy in heads + [rows_copy, c_copy, wo_copy, bk_copy]:
         copy.wait_send()
@@ -554,27 +585,20 @@
         r1_copy(k).wait_send()
     for k in line_order:
         rz_copy(k).wait_send()
-
-        @pl.when(sums(k))
-        def _(k=k):
-            r2_copy(k).wait_send()
+        r2_copy(k).wait_send()
+        f_copy(k).wait_send()
 
     for k in plane_order:
+        r3_copy(k).wait_send()
 
         @pl.when(wants(k))
         def _(k=k):
-            r3_copy(k).wait_send()
-
-    @pl.when(sums(0))
-    def _():
-        for k in line_order:
-            f_copy(k).wait_send()
+            e3_copy(k).wait_send()
 
     @pl.when(holder)
     def _():
         for k in line_order:
             zg_copy(k).wait_send()
-        own_z.wait()
 
     for k in LINE:
 
@@ -586,29 +610,37 @@
         ag_copy(k).wait_send()
     for k in [0] + mates:
         ad_copy(k).wait_send()
-    own_p.wait()
-    for copy in gs_copies:
+    for copy in gs_copies + gw_copies:
         copy.wait()
 
 
-def finish(gw, gs_i, gs_t, out_hi, out_ht, out_i, out_t, narrow, wide, in_s, out_s, gs_s):
+def finish(gw, gs_i, gs_t, out_hi, out_ht, out_i, out_t, narrow, wide, held, in_s, out_s, gi_s, go_s):
     loads = [pltpu.make_async_copy(gw.at[m], narrow.at[m], in_s.at[m]) for m in range(2)]
+    moves = []
+    for m, (src, dst) in enumerate(((gs_i, out_i), (gs_t, out_t))):
+        at = held.at[m]
+        moves.append(
+            (
+                pltpu.make_async_copy(src, at, gi_s.at[m]),
+                pltpu.make_async_copy(at, dst, go_s.at[m]),
+            )
+        )
+    moves[0][0].start()
     for copy in loads:
         copy.start()
-    step = S // 4
-    copies = []
-    for m, (src, dst) in enumerate(((gs_i, out_i), (gs_t, out_t))):
-        for n in range(4):
-            at = pl.ds(n * step, step)
-            copies.append(pltpu.make_async_copy(src.at[at, :], dst.at[at, :], gs_s.at[4 * m + n]))
-    for copy in copies:
-        copy.start()
-    for m, dst in enumerate((out_hi, out_ht)):
+    moves[1][0].start()
+    stores = [pltpu.make_async_copy(wide.at[m], dst, out_s.at[m]) for m, dst in enumerate((out_hi, out_ht))]
+    moves[0][0].wait()
+    moves[0][1].start()
+    for m in range(2):
         loads[m].wait()
         wide[m] = narrow[m].astype(F32)
-        copies.append(pltpu.make_async_copy(wide.at[m], dst, out_s.at[m]))
-        copies[-1].start()
-    for copy in copies:
+        stores[m].start()
+    moves[1][0].wait()
+    moves[1][1].start()
+    for copy in stores:
+        copy.wait()
+    for _, copy in moves:
         copy.wait()
 
 
@@ -630,14 +662,15 @@
         space((NZ * N2, E)), space((2 * PLANE * N, E)),
         space((N2, E)), space((N, E)), space((2, S, D), F32), space((D, E), F32),
         space((PLANE * PIECE, E)), space((NZ * PIECE, E)), space((PLANE * PIECE, E)),
-        space((NZ * PIECE, E)), space((PLANE * PIECE, E)), space((PIECE, E)), space((PIECE, E)),
-        space((PIECE, E)), space((NZ * 16, E)), space((PIECE, E)), space((16, E)),
+        space((NZ * PIECE, E)), space((TILES * 16, 128)), space((TILES * 16, 128)), space((16, 128)),
+        space((TILES * 16, 128)), space((PIECE, E)), space((TILES * 16, 128)), space((TILES * 16, 128)),
+        space((32, 128)), space((TILES * 16, 128)), space((PIECE, E)), space((2, H, E)),
     ]
     counts = [
         3, 2, 2, 0, 0, 0, 0, 0, 0,
         NZ, NZ, NZ, 2 * PLANE, PLANE, NZ, NZ, NZ, NZ, PLANE, 2 * PLANE,
-        0, 0, 2, PLANE, PLANE, NZ, NZ, PLANE, PLANE, NZ, NZ, NZ, NZ,
-        NZ, NZ, NZ, NZ, 2, PLANE, PLANE, PLANE, PLANE,
+        0, 0, 2, PLANE, PLANE, NZ, NZ, PLANE, PLANE, PLANE, PLANE, NZ, NZ, NZ, NZ,
+        NZ, NZ, NZ, NZ, 2, 2, PLANE, PLANE, PLANE, PLANE,
     ]
     sems = [dma((n,)) if n else dma for n in counts]
     gs_i, gs_t, gw = pl.pallas_call(
@@ -662,7 +695,11 @@
         out_shape=(jax.ShapeDtypeStruct((H, E), F32),) * 2 + (jax.ShapeDtypeStruct((S, D), F32),) * 2,
         in_specs=[hbm] * 3,
         out_specs=(hbm,) * 4,
-        scratch_shapes=[space((2, H, E)), space((2, H, E), F32), dma((2,)), dma((2,)), dma((8,))],
+        scratch_shapes=[
+            space((2, H, E)), space((2, H, E), F32), space((2, S, D), F32),
+            dma((2,)), dma((2,)), dma((2,)), dma((2,)),
+        ],
+        compiler_params=pltpu.CompilerParams(vmem_limit_bytes=60 * 1024 * 1024),
     )(gw, gs_i, gs_t)
 
 

time: 202 us -> 110 us (0.54)
  Pallas kernels: 199 us -> 107 us
    pallas_call x1, Pallas kernels: 90.6 us -> 4.01 us  [body(): pl.pallas_call(finish, out_shape=(jax.ShapeDtypeStruct((H, E), F32),) * 2...]
    pallas_call x1, Pallas kernels: 108 us -> 103 us  [body(): pl.pallas_call(kernel, out_shape=(jax.ShapeDtypeStruct((S, D), F32), jax....]
where the time goes in v4:
time: 110 us
  Pallas kernels  107 us (97%)
  between operations  2.58 us (2%)
    pallas_call x1, Pallas kernels, body(): pl.pallas_call(kernel, out_shape=(jax.ShapeDtypeStruct((S, D), F32), jax....  103 us
    pallas_call x1, Pallas kernels, body(): pl.pallas_call(finish, out_shape=(jax.ShapeDtypeStruct((H, E), F32),) * 2...  4.01 us

profile of v4, /device:TPU:35, one launch (start us, length us, event | category | flops | bytes accessed | tf_op | source)
XLA Modules:
  0.0 109.8 jit_solution(3145830580767689656)
XLA Ops:
  2.6 103.2 %shard_map.129 = (f32[320,1152]{1,0:T(8,128)}, f32[320,1152]{1,0:T(8,128)}, bf16[2,576,576]{2,1,0:T(8,128)(2,1)}) custom-call(bf16[320,1152]{1,0:T(8,128)(2,1)} %sup_i.1, bf16[320,1152]{1,0:T(8,128)(2,1)} %sup_t.1, s32[1,64]{1,0:T(1,128)} %bitcast.9, s32[1,64]{1,0:T(1,128)} %bitcast.10, f32[1,16]{1,0:T(1,128)} %bitcast.11, bf16[576,576]{1,0:T(8,128)(2,1)} %head_i.1, ...), custom_call_target="tpu_custom_call" | custom-call | tf_op jit(solution)/shard_map/pallas_call | solution.py:676
  105.8 4.0 %shard_map.130 = (f32[576,576]{1,0:T(8,128)}, f32[576,576]{1,0:T(8,128)}, f32[320,1152]{1,0:T(8,128)}, f32[320,1152]{1,0:T(8,128)}) custom-call(bf16[2,576,576]{2,1,0:T(8,128)(2,1)} %get-tuple-element.7.gw, f32[320,1152]{1,0:T(8,128)} %get-tuple-element.8.gs_i, f32[320,1152]{1,0:T(8,128)} %get-tuple-element.9.gs_t), custom_call_target="tpu_custom_call" | custom-call | tf_op jit(solution)/shard_map/pallas_call | solution.py:693

commit v5 on v4

--- a/solution.py
+++ b/solution.py
@@ -36,7 +36,8 @@
     return (-(k // NY)) % NX * NY + (-(k % NY)) % NY
 
 
-LINE = (0, 1, 7, 2, 6, 3, 5, 4)
+LINE = (0, 2, 6, 1, 7, 3, 5, 4)
+RING = (0, 1, 3, 2)
 SHEET = tuple(sorted(range(PLANE), key=lambda k: (hops(k), k)))
 
 
@@ -61,10 +62,11 @@
     sup_i, sup_t, sel, bkt, wts, head_i, head_t, lscale, lbias, oscale,
     gs_i, gs_t, gw,
     va, vt, a, stage, cbuf, wfull, wother, unit, length,
-    em, img, txt, g, p_f, p_out, p_in, t_out, rs_i, rs_t,
+    em, img, txt, g, p_f, p_out, p_in, t_out, t_own, rv_in, u_out, rs_a, rs_b, rs_i, rs_t,
     bk, bo, gsv, dwf, dws, dwz, r1, rz, r3, zsum, zres, zft, zfin, psum, r2, res, fint, fin, gwv,
     in_s, w_s, w_r, rows_s, rows_r, c_s, c_r, wo_s, wo_r,
-    ia_s, ia_r, if_s, ta_s, ta_r, pi_s, pi_r, ri_s, ri_r, rt_s, rt_r,
+    ia_s, ia_r, ip_s, if_s, ta_s, ta_r, tp_s, pi_s, pi_r, ri_s, ri_r, ra_r, rb_s, rb_r,
+    rv_s, rv_r, ru_s, ru_r,
     bk_s, bk_r, gs_s, r1_s, r1_r, rz_s, rz_r, r3_s, r3_r, e3_s, e3_r, r2_s, r2_r, f_s, f_r,
     zg_s, zg_r, zd_s, zd_r, own_s, gw_s, ag_s, ag_r, ad_s, ad_r,
 ):
@@ -181,41 +183,74 @@
 
     line_order, plane_order = LINE[1:], SHEET[1:]
 
+    def ahead(at, k, size):
+        return lax.rem(at + k, size)
+
+    def u_peer(k, c=core):
+        return device(
+            jnp.where(first, ahead(x, k, NX), x), jnp.where(first, y, ahead(y, k, NY)), z, c
+        )
+
+    def v_peer(k):
+        return device(
+            jnp.where(first, x, ahead(x, k, NX)), jnp.where(first, ahead(y, k, NY), y), z, core
+        )
+
     def img_at(k):
         return LINE.index(k % NZ) * N2
 
-    def txt_at(k):
-        return SHEET.index(k) * N
+    def txt_at(u, v):
+        return (RING.index(v % 4) * 4 + RING.index(u % 4)) * N
 
     def ia(k):
-        return remote(
-            em, rows(img, img_at(-k), N2), ia_s.at[k], ia_r.at[(NZ - k) % NZ], line(k)
+        return remote(em, rows(img, img_at(-k), N2), ia_s.at[k], ia_r.at[(NZ - k) % NZ], line(k))
+
+    def ip(k):
+        step = 1 if k == 6 else NZ - 1
+        src = rows(img, img_at(k), N2)
+        off, n = (0, 4) if k == 2 else (N, NZ)
+        return (
+            remote(src, rows(img, img_at(k - step), N2), ip_s.at[k], ia_r.at[(k - step) % NZ], line(step)),
+            remote(
+                rows(img, img_at(k) + off, N), rows(img, img_at(4) + off, N),
+                ip_s.at[(k + 1) % NZ], ia_r.at[n], line((NZ - k) % NZ),
+            ),
         )
 
     def fwd(k):
         block = rows(img, img_at(k), N2)
         return remote(em if k == 0 else block, block, if_s.at[k], ia_r.at[k], sib)
 
-    def ta(k, c):
-        return remote(
-            rows(em, c * N, N), rows(txt, txt_at(back_slot(k)), N),
-            ta_s.at[2 * k + c], ta_r.at[back_slot(k)], plane(k, c),
+    def ta0(k):
+        to = device(ahead(x, k, NX), y, z, 0)
+        return remote(rows(em, 0, N), rows(txt, txt_at(-k, 0), N), ta_s.at[k], ta_r.at[(-k) % 4], to)
+
+    def ta1(k):
+        to = device(x, ahead(y, k, NY), z, 1)
+        return remote(
+            rows(em, N, N), rows(txt, txt_at(-k, 0), N), ta_s.at[4 + k], ta_r.at[(-k) % 4], to
+        )
+
+    def tp(u, v):
+        return remote(
+            rows(txt, txt_at(u, 0), N), rows(txt, txt_at(u, -v), N),
+            tp_s.at[4 * v + u], ta_r.at[(-v) % 4 * 4 + u], v_peer(v),
         )
 
     @pl.when(first)
     def _():
-        for k in line_order:
+        for k in line_order[:4]:
             ia(k).start()
         fwd(0).start()
         img[0:N2, :] = em[...]
 
     @pl.when(core == 1)
     def _():
-        ta(0, 0).start()
-        for k in plane_order:
-            ta(k, 0).start()
-            ta(k, 1).start()
         txt[0:N, :] = em[N:N2, :]
+        for k in RING[::-1]:
+            ta0(k).start()
+            if k:
+                ta1(k).start()
 
     wo_copy = remote(wfull, wother, wo_s, wo_r, sib)
     wo_copy.start()
@@ -226,22 +261,33 @@
     def take_image(k):
         @pl.when(first)
         def _():
+            if k == 4:
+                for n in range(2):
+                    arrived(rows(img, img_at(4) + n * N, N), ia_r.at[4 + 4 * n], ia_s.at[0])
+            elif k:
+                arrived(rows(img, img_at(k), N2), ia_r.at[k], ia_s.at[0])
+            if k in (2, 6):
+                for copy in ip(k):
+                    copy.start()
             if k:
-                arrived(rows(img, img_at(k), N2), ia_r.at[k], ia_s.at[0])
                 fwd(k).start()
 
         @pl.when(core == 1)
         def _():
             arrived(rows(img, img_at(k), N2), ia_r.at[k], ia_s.at[0])
 
-    def take_text(k):
-        if k:
-            arrived(rows(txt, txt_at(k), N), ta_r.at[k], ta_s.at[0])
+    def take_text(u, v):
+        if u or v:
+            arrived(rows(txt, txt_at(u, v), N), ta_r.at[4 * v + u], ta_s.at[0])
         else:
 
             @pl.when(first)
             def _():
                 arrived(rows(txt, 0, N), ta_r.at[0], ta_s.at[0])
+
+        if v == 0:
+            for k in RING[:0:-1]:
+                tp(u, k).start()
 
     def tile(i, j, diagonal=False):
         block = img[pl.ds(pl.multiple_of(i * B, B), B), :]
@@ -256,8 +302,8 @@
         g[pl.ds(pl.multiple_of(i * B, B), B), pl.ds(pl.multiple_of(j * B, B), B)] = value.astype(BF)
 
     for t in range(NZ * N2 // B):
-        for k in SHEET[4 * t : 4 * t + 4]:
-            take_text(k)
+        for u in RING:
+            take_text(u, RING[t])
         for k in LINE[2 * t : 2 * t + 2]:
             take_image(k)
         tile(t, t, t == 0)
@@ -274,28 +320,56 @@
         )
 
     def ri(k):
-        return remote(
-            rows(p_out, img_at(k), N2), rows(rs_i, (NZ - k) % NZ * N2, N2),
-            ri_s.at[k], ri_r.at[(NZ - k) % NZ], line(k),
-        )
-
-    def rt(k):
-        return remote(
-            rows(t_out, txt_at(k), N), rows(rs_t, (core * PLANE + back_slot(k)) * N, N),
-            rt_s.at[k], rt_r.at[core * PLANE + back_slot(k)], plane(k, 1),
-        )
+        src = rows(p_out, img_at(k), N2)
+        if k in (3, 5):
+            n = 0 if k == 3 else 1
+            return [remote(src, rows(rs_a, n * N2, N2), ri_s.at[k], ra_r.at[n], line(1 if k == 3 else 7))]
+        if k == 4:
+            return [
+                remote(
+                    rows(p_out, img_at(4) + n * N, N), rows(rs_b, n * N, N),
+                    rb_s.at[n], rb_r.at[n], line((2, 6)[n]),
+                )
+                for n in range(2)
+            ]
+        back_k = (NZ - k) % NZ
+        return [remote(src, rows(rs_i, back_k * N2, N2), ri_s.at[k], ri_r.at[back_k], line(k))]
 
     def combine(k):
         at = img_at(k)
         arrived(rows(p_in, at, N2), pi_r.at[k], pi_s.at[k])
         total = p_f[at : at + N2, :] + p_in[at : at + N2, :].astype(F32)
+        if k in (2, 6):
+            n = (2, 6).index(k)
+            arrived(rows(rs_a, n * N2, N2), ra_r.at[n], ri_s.at[0])
+            total += rs_a[n * N2 : (n + 1) * N2, :].astype(F32)
+            arrived(rows(rs_b, n * N, N), rb_r.at[n], rb_s.at[n])
+            more = rs_b[n * N : (n + 1) * N, :].astype(F32)
+            half_of = total[n * N : (n + 1) * N, :] + more
+            keep = total[(1 - n) * N : (2 - n) * N, :]
+            total = jnp.concatenate([half_of, keep] if n == 0 else [keep, half_of], axis=0)
         if k:
             p_out[at : at + N2, :] = total.astype(BF)
-            ri(k).start()
+            for copy in ri(k):
+                copy.start()
         else:
             p_f[0:N2, :] = total
 
-    back_order = LINE[::-1]
+    def rv(v):
+        n = RING.index(v) * 4 * N
+        return remote(
+            rows(t_out, n, 4 * N), rows(rv_in, (-v) % 4 * 4 * N, 4 * N),
+            rv_s.at[v], rv_r.at[(-v) % 4], v_peer(v),
+        )
+
+    def ru(u):
+        at = core * 4 + (-u) % 4
+        return remote(
+            rows(u_out, u * N, N), rows(rs_t, at * N, N), ru_s.at[u], ru_r.at[at], u_peer(u, 1)
+        )
+
+    back_order = (4, 3, 5, 1, 7, 2, 6, 0)
+    text_order = (2, 1, 3, 0)
     for n in range(NZ + 1):
         if n < NZ:
             k = back_order[n]
@@ -307,34 +381,57 @@
                 p_out[at : at + N2, :] = p_f[at : at + N2, :].astype(BF)
                 pi(k).start()
 
-            b = NZ - 1 - n
+            v = text_order[n // 2]
+            b = 2 * RING.index(v) + n % 2
             block = dot(g[:, b * N2 : (b + 1) * N2], img[:, 0:E], ((0,), (0,)))
-            t_out[b * N2 : (b + 1) * N2, :] = block.astype(BF)
-            for k in SHEET[2 * b : 2 * b + 2]:
-                if k:
-                    rt(k).start()
+            if v:
+                t_out[b * N2 : (b + 1) * N2, :] = block.astype(BF)
+            else:
+                t_own[b * N2 : (b + 1) * N2, :] = block
+            if v and n % 2:
+                rv(v).start()
         if n:
 
             @pl.when(first)
             def _(n=n):
                 combine(back_order[n - 1])
 
+    for v in text_order[:3]:
+        arrived(rows(rv_in, v * 4 * N, 4 * N), rv_r.at[v], rv_s.at[v])
+    for u in RING[::-1]:
+        at = RING.index(u) * N
+        total = t_own[at : at + N, :]
+        for v in (1, 2, 3):
+            row = v * 4 * N + at
+            total += rv_in[row : row + N, :].astype(F32)
+        if u:
+            u_out[u * N : (u + 1) * N, :] = total.astype(BF)
+            ru(u).start()
+        else:
+
+            @pl.when(first)
+            def _(total=total):
+                u_out[0:N, :] = total.astype(BF)
+                remote(rows(u_out, 0, N), rows(rs_t, 0, N), ru_s.at[0], ru_r.at[0], sib).start()
+
+            @pl.when(core == 1)
+            def _(total=total):
+                p_f[N:N2, :] = total
+
     @pl.when(first)
     def _():
-        rt(0).start()
-        for k in line_order:
+        for k in (1, 7, 2, 6):
             arrived(rows(rs_i, k * N2, N2), ri_r.at[k], ri_s.at[0])
             p_f[0:N2, :] += rs_i[k * N2 : (k + 1) * N2, :].astype(F32)
 
     @pl.when(core == 1)
-    def _(block=block):
-        arrived(rows(rs_t, 0, N), rt_r.at[0], rt_s.at[0])
+    def _():
+        arrived(rows(rs_t, 0, N), ru_r.at[0], ru_s.at[0])
         p_f[0:N, :] = rs_t[0:N, :].astype(F32)
-        p_f[N:N2, :] = block[0:N, :]
-        for k in plane_order:
+        for k in RING[1:]:
             for c in range(2):
-                at = c * PLANE + k
-                arrived(rows(rs_t, at * N, N), rt_r.at[at], rt_s.at[0])
+                at = c * 4 + k
+                arrived(rows(rs_t, at * N, N), ru_r.at[at], ru_s.at[0])
                 p_f[c * N : (c + 1) * N, :] += rs_t[at * N : (at + 1) * N, :].astype(F32)
 
     grad = p_f[0:N2, :] * scale
@@ -564,24 +661,33 @@
 
     @pl.when(first)
     def _():
+        for k in line_order[:4]:
+            ia(k).wait_send()
+        for k in (2, 6):
+            for copy in ip(k):
+                copy.wait_send()
         for k in line_order:
-            ia(k).wait_send()
-            ri(k).wait_send()
+            for copy in ri(k):
+                copy.wait_send()
         for k in LINE:
             fwd(k).wait_send()
-        rt(0).wait_send()
+        remote(rows(u_out, 0, N), rows(rs_t, 0, N), ru_s.at[0], ru_r.at[0], sib).wait_send()
 
     @pl.when(core == 1)
     def _():
         for k in LINE:
             pi(k).wait_send()
-        ta(0, 0).wait_send()
-        for k in plane_order:
-            ta(k, 0).wait_send()
-            ta(k, 1).wait_send()
-
+        for k in RING:
+            ta0(k).wait_send()
+            if k:
+                ta1(k).wait_send()
+
+    for k in RING[1:]:
+        for u in RING:
+            tp(u, k).wait_send()
+        rv(k).wait_send()
+        ru(k).wait_send()
     for k in plane_order:
-        rt(k).wait_send()
         r1_copy(k).wait_send()
     for k in line_order:
         rz_copy(k).wait_send()
@@ -659,7 +765,8 @@
         space((N2, EP)), space((NZ * N2, EP)), space((PLANE * N, EP)),
         space((NZ * N2, PLANE * N)),
         space((NZ * N2, E), F32), space((NZ * N2, E)), space((NZ * N2, E)), space((PLANE * N, E)),
-        space((NZ * N2, E)), space((2 * PLANE * N, E)),
+        space((4 * N, E), F32), space((PLANE * N, E)), space((4 * N, E)), space((2 * N2, E)), space((N2, E)),
+        space((NZ * N2, E)), space((8 * N, E)),
         space((N2, E)), space((N, E)), space((2, S, D), F32), space((D, E), F32),
         space((PLANE * PIECE, E)), space((NZ * PIECE, E)), space((PLANE * PIECE, E)),
         space((NZ * PIECE, E)), space((TILES * 16, 128)), space((TILES * 16, 128)), space((16, 128)),
@@ -668,7 +775,7 @@
     ]
     counts = [
         3, 2, 2, 0, 0, 0, 0, 0, 0,
-        NZ, NZ, NZ, 2 * PLANE, PLANE, NZ, NZ, NZ, NZ, PLANE, 2 * PLANE,
+        NZ, NZ + 1, NZ, NZ, 8, PLANE, PLANE, NZ, NZ, NZ, NZ, 2, 2, 2, 4, 4, 4, 8,
         0, 0, 2, PLANE, PLANE, NZ, NZ, PLANE, PLANE, PLANE, PLANE, NZ, NZ, NZ, NZ,
         NZ, NZ, NZ, NZ, 2, 2, PLANE, PLANE, PLANE, PLANE,
     ]

time: 110 us -> 105 us (0.955)
  Pallas kernels: 107 us -> 102 us
    pallas_call x1, Pallas kernels: 103 us -> 98 us  [body(): pl.pallas_call(kernel, out_shape=(jax.ShapeDtypeStruct((S, D), F32), jax....]
where the time goes in v5:
time: 105 us
  Pallas kernels  102 us (97%)
  between operations  2.58 us (2%)
    pallas_call x1, Pallas kernels, body(): pl.pallas_call(kernel, out_shape=(jax.ShapeDtypeStruct((S, D), F32), jax....  98 us
    pallas_call x1, Pallas kernels, body(): pl.pallas_call(finish, out_shape=(jax.ShapeDtypeStruct((H, E), F32),) * 2...  4.01 us

profile of v5, /device:TPU:35, one launch (start us, length us, event | category | flops | bytes accessed | tf_op | source)
XLA Modules:
  0.0 104.5 jit_solution(17855030575380440239)
XLA Ops:
  2.6 98.0 %shard_map.129 = (f32[320,1152]{1,0:T(8,128)}, f32[320,1152]{1,0:T(8,128)}, bf16[2,576,576]{2,1,0:T(8,128)(2,1)}) custom-call(bf16[320,1152]{1,0:T(8,128)(2,1)} %sup_i.1, bf16[320,1152]{1,0:T(8,128)(2,1)} %sup_t.1, s32[1,64]{1,0:T(1,128)} %bitcast.9, s32[1,64]{1,0:T(1,128)} %bitcast.10, f32[1,16]{1,0:T(1,128)} %bitcast.11, bf16[576,576]{1,0:T(8,128)(2,1)} %head_i.1, ...), custom_call_target="tpu_custom_call" | custom-call | tf_op jit(solution)/shard_map/pallas_call | solution.py:783
  100.5 4.0 %shard_map.130 = (f32[576,576]{1,0:T(8,128)}, f32[576,576]{1,0:T(8,128)}, f32[320,1152]{1,0:T(8,128)}, f32[320,1152]{1,0:T(8,128)}) custom-call(bf16[2,576,576]{2,1,0:T(8,128)(2,1)} %get-tuple-element.7.gw, f32[320,1152]{1,0:T(8,128)} %get-tuple-element.8.gs_i, f32[320,1152]{1,0:T(8,128)} %get-tuple-element.9.gs_t), custom_call_target="tpu_custom_call" | custom-call | tf_op jit(solution)/shard_map/pallas_call | solution.py:800

commit v6 on v5

--- a/solution.py
+++ b/solution.py
@@ -301,11 +301,16 @@
             value = jnp.where((r == c + core * N) & (c < N), -value * e, value)
         g[pl.ds(pl.multiple_of(i * B, B), B), pl.ds(pl.multiple_of(j * B, B), B)] = value.astype(BF)
 
+    for u in RING:
+        take_text(u, 0)
+    for k in LINE[:3]:
+        take_image(k)
     for t in range(NZ * N2 // B):
-        for u in RING:
-            take_text(u, RING[t])
-        for k in LINE[2 * t : 2 * t + 2]:
-            take_image(k)
+        if t:
+            for k in LINE[max(2 * t, 3) : 2 * t + 2]:
+                take_image(k)
+            for u in RING:
+                take_text(u, RING[t])
         tile(t, t, t == 0)
         if t:
 

time: 105 us -> 101 us (0.962)
  Pallas kernels: 102 us -> 98 us
    pallas_call x1, Pallas kernels: 98 us -> 94 us  [body(): pl.pallas_call(kernel, out_shape=(jax.ShapeDtypeStruct((S, D), F32), jax....]
where the time goes in v6:
time: 101 us
  Pallas kernels  98 us (97%)
  between operations  2.58 us (3%)
    pallas_call x1, Pallas kernels, body(): pl.pallas_call(kernel, out_shape=(jax.ShapeDtypeStruct((S, D), F32), jax....  94 us
    pallas_call x1, Pallas kernels, body(): pl.pallas_call(finish, out_shape=(jax.ShapeDtypeStruct((H, E), F32),) * 2...  4.01 us

profile of v6, /device:TPU:35, one launch (start us, length us, event | category | flops | bytes accessed | tf_op | source)
XLA Modules:
  0.0 100.6 jit_solution(11602205863551743746)
XLA Ops:
  2.6 94.0 %shard_map.129 = (f32[320,1152]{1,0:T(8,128)}, f32[320,1152]{1,0:T(8,128)}, bf16[2,576,576]{2,1,0:T(8,128)(2,1)}) custom-call(bf16[320,1152]{1,0:T(8,128)(2,1)} %sup_i.1, bf16[320,1152]{1,0:T(8,128)(2,1)} %sup_t.1, s32[1,64]{1,0:T(1,128)} %bitcast.9, s32[1,64]{1,0:T(1,128)} %bitcast.10, f32[1,16]{1,0:T(1,128)} %bitcast.11, bf16[576,576]{1,0:T(8,128)(2,1)} %head_i.1, ...), custom_call_target="tpu_custom_call" | custom-call | tf_op jit(solution)/shard_map/pallas_call | solution.py:788
  96.6 4.0 %shard_map.130 = (f32[576,576]{1,0:T(8,128)}, f32[576,576]{1,0:T(8,128)}, f32[320,1152]{1,0:T(8,128)}, f32[320,1152]{1,0:T(8,128)}) custom-call(bf16[2,576,576]{2,1,0:T(8,128)(2,1)} %get-tuple-element.7.gw, f32[320,1152]{1,0:T(8,128)} %get-tuple-element.8.gs_i, f32[320,1152]{1,0:T(8,128)} %get-tuple-element.9.gs_t), custom_call_target="tpu_custom_call" | custom-call | tf_op jit(solution)/shard_map/pallas_call | solution.py:805

commit v7 on v6

--- a/solution.py
+++ b/solution.py
@@ -98,6 +98,14 @@
     def greet(to):
         pl.semaphore_signal(barrier, inc=1, device_id=to, device_id_type=MESH)
 
+    for k in SHEET[:0:-1]:
+        greet(plane(k))
+    for k in LINE[:0:-1]:
+        greet(line(k))
+    for k in range(NY, PLANE, NY):
+        greet(plane(k, 1 - core))
+    greet(sib)
+
     h_off = pl.multiple_of(half * H, H)
     sup_copies = [
         pltpu.make_async_copy(sup_i, va, in_s.at[0]),
@@ -114,13 +122,6 @@
     @pl.when(core == 1)
     def _():
         pltpu.make_async_copy(head_t, rows(wfull, h_off, H), in_s.at[2]).start()
-
-    greet(sib)
-    for k in range(1, NZ):
-        greet(line(k))
-    for k in range(1, PLANE):
-        greet(plane(k, 0))
-        greet(plane(k, 1))
 
     for copy in sup_copies:
         copy.wait()
@@ -139,7 +140,7 @@
     )
 
     head_copy.wait()
-    pl.semaphore_wait(barrier, 1 + (NZ - 1) + 2 * (PLANE - 1))
+    pl.semaphore_wait(barrier, 1 + (NZ - 1) + (PLANE - 1) + (NX - 1))
 
     heads = []
     for k, step in ((0, 1), (1, NX - 1)):

time: 101 us -> 100 us (0.990)
  no operation moved by 1% of the time
where the time goes in v7:
time: 100 us
  Pallas kernels  97.5 us (98%)
  between operations  2.58 us (3%)
    pallas_call x1, Pallas kernels, body(): pl.pallas_call(kernel, out_shape=(jax.ShapeDtypeStruct((S, D), F32), jax....  93.5 us
    pallas_call x1, Pallas kernels, body(): pl.pallas_call(finish, out_shape=(jax.ShapeDtypeStruct((H, E), F32),) * 2...  4.01 us

profile of v7, /device:TPU:35, one launch (start us, length us, event | category | flops | bytes accessed | tf_op | source)
XLA Modules:
  0.0 100.1 jit_solution(3875599910752239988)
XLA Ops:
  2.6 93.5 %shard_map.129 = (f32[320,1152]{1,0:T(8,128)}, f32[320,1152]{1,0:T(8,128)}, bf16[2,576,576]{2,1,0:T(8,128)(2,1)}) custom-call(bf16[320,1152]{1,0:T(8,128)(2,1)} %sup_i.1, bf16[320,1152]{1,0:T(8,128)(2,1)} %sup_t.1, s32[1,64]{1,0:T(1,128)} %bitcast.9, s32[1,64]{1,0:T(1,128)} %bitcast.10, f32[1,16]{1,0:T(1,128)} %bitcast.11, bf16[576,576]{1,0:T(8,128)(2,1)} %head_i.1, ...), custom_call_target="tpu_custom_call" | custom-call | tf_op jit(solution)/shard_map/pallas_call | solution.py:789
  96.1 4.0 %shard_map.130 = (f32[576,576]{1,0:T(8,128)}, f32[576,576]{1,0:T(8,128)}, f32[320,1152]{1,0:T(8,128)}, f32[320,1152]{1,0:T(8,128)}) custom-call(bf16[2,576,576]{2,1,0:T(8,128)(2,1)} %get-tuple-element.7.gw, f32[320,1152]{1,0:T(8,128)} %get-tuple-element.8.gs_i, f32[320,1152]{1,0:T(8,128)} %get-tuple-element.9.gs_t), custom_call_target="tpu_custom_call" | custom-call | tf_op jit(solution)/shard_map/pallas_call | solution.py:806
